TPU v7x, 512 devices: a whole 4x8x8 slice. The times are simulated.
512 devices in a mesh: tok: 32 (over x, z), img: 16 (over y, core).
Axes of the slice: x: 4, y: 8, z: 8, core: 2. Of those that a mesh axis runs over, the one named last changes fastest.
Arguments:
- query_in: bfloat16 [2, 16, 4096, 1120], P(None, 'img', 'tok'), may hold values from -6 to 6
- key_in: bfloat16 [2, 16, 4096, 1120], P(None, 'img', 'tok'), may hold values from -6 to 6
- value_in: bfloat16 [2, 16, 4096, 1120], P(None, 'img', 'tok'), may hold values from -6 to 6
- cotangent: bfloat16 [2, 16, 4096, 1152], P(None, 'img', 'tok'), may hold values from -6 to 6
- out_weight: bfloat16 [1120, 1152], P('tok', 'img'), may hold values from -0.1875 to 0.1875
- gate_table: float32 [1152], replicated, may hold values from -6 to 6
- time_gate: float32 [2, 16, 1152], P(None, 'img'), may hold values from -6 to 6
Outputs:
- query_grad: bfloat16 [2, 16, 4096, 1120], P(None, 'img', 'tok')
- key_grad: bfloat16 [2, 16, 4096, 1120], P(None, 'img', 'tok')
- value_grad: bfloat16 [2, 16, 4096, 1120], P(None, 'img', 'tok')
- gate_grad: float32 [1152], P('img')
- weight_grad: float32 [1120, 1152], P('tok', 'img')
All inputs are finite; a program needn't handle non-finite values.
Results may differ from a plain program's by a relative error of at most 0.022.
Values may be sent and summed in bfloat16 or wider, within the bound.
A program may use at most 64 MiB of HBM per device.

v0:
```python
import jax
import jax.numpy as jnp
from jax import lax
from jax.sharding import PartitionSpec as P

HEAD = 112
LOSS_SCALE = 1024


def kernel(values_in):
    return jnp.where(values_in > 0, values_in + 1.0, jnp.exp(jnp.minimum(values_in, 0.0)))


def kernel_slope(values_in):
    return jnp.where(values_in > 0, 1.0, jnp.exp(jnp.minimum(values_in, 0.0)))


def on_device(query_in, key_in, value_in, cotangent, out_weight, gate_table, time_gate):
    highest = lax.Precision.HIGHEST
    step_count = query_in.shape[0]
    tok_rows = query_in.shape[2]
    feat_count = query_in.shape[3]
    head_count = feat_count // HEAD
    row_block = lax.all_gather(out_weight, "tok", axis=0, tiled=True)
    weight_full = lax.all_gather(row_block, "img", axis=1, tiled=True)
    out_count = weight_full.shape[1]
    split_shape = (step_count, tok_rows, head_count, HEAD)
    query_f = query_in[:, 0].astype(jnp.float32).reshape(split_shape)
    key_f = key_in[:, 0].astype(jnp.float32).reshape(split_shape)
    value_f = value_in[:, 0].astype(jnp.float32).reshape(split_shape)
    kern_q = kernel(query_f)
    kern_k = kernel(key_f)
    state_part = jnp.einsum("sthe,sthf->shef", kern_k, value_f, precision=highest)
    keysum_part = jnp.sum(kern_k, axis=1)
    summed = []
    for step_idx in range(step_count):
        summed.append(lax.psum((state_part[step_idx], keysum_part[step_idx]), "tok"))
    state = jnp.stack([member[0] for member in summed])
    key_sum = jnp.stack([member[1] for member in summed])
    numerator = jnp.einsum("sthe,shef->sthf", kern_q, state, precision=highest)
    denominator = jnp.einsum("sthe,she->sth", kern_q, key_sum, precision=highest)
    attn_ratio = numerator / denominator[..., None]
    attended = attn_ratio.astype(jnp.bfloat16).reshape(step_count * tok_rows, feat_count)
    projected = jnp.dot(attended, weight_full, preferred_element_type=jnp.float32)
    projected = projected.reshape(step_count, tok_rows, out_count)
    cotan_f = cotangent[:, 0].astype(jnp.float32)
    local_gate = jnp.sum(cotan_f * projected, axis=(0, 1))
    gate_full = gate_table[None, :] + time_gate[:, 0, :]
    scaled = (LOSS_SCALE * gate_full[:, None, :] * cotan_f).astype(jnp.bfloat16)
    scaled = scaled.reshape(step_count * tok_rows, out_count)
    band_sum = lax.dot_general(
        attended, scaled, (((0,), (0,)), ((), ())), preferred_element_type=jnp.float32
    )
    tok_share = lax.psum_scatter(
        band_sum.astype(jnp.bfloat16), "tok", scatter_dimension=0, tiled=True
    ).astype(jnp.float32)
    weight_grad = lax.psum_scatter(tok_share, "img", scatter_dimension=1, tiled=True) / LOSS_SCALE
    d_attended = lax.dot_general(
        scaled, weight_full, (((1,), (1,)), ((), ())), preferred_element_type=jnp.float32
    )
    d_attended = d_attended.reshape(split_shape)
    d_numer = d_attended / denominator[..., None]
    d_denom = -jnp.sum(d_numer * attn_ratio, axis=-1)
    dstate_part = jnp.einsum("sthe,sthf->shef", kern_q, d_numer, precision=highest)
    dkeysum_part = jnp.einsum("sthe,sth->she", kern_q, d_denom, precision=highest)
    grads_summed = []
    for step_idx in range(step_count):
        grads_summed.append(lax.psum((dstate_part[step_idx], dkeysum_part[step_idx]), "tok"))
    d_state = jnp.stack([member[0] for member in grads_summed])
    d_keysum = jnp.stack([member[1] for member in grads_summed])
    d_kernq = (
        jnp.einsum("sthf,shef->sthe", d_numer, state, precision=highest)
        + d_denom[..., None] * key_sum[:, None]
    )
    d_kernk = jnp.einsum("sthf,shef->sthe", value_f, d_state, precision=highest) + d_keysum[:, None]
    d_value = jnp.einsum("sthe,shef->sthf", kern_k, d_state, precision=highest)
    out_shape = (step_count, 1, tok_rows, feat_count)
    query_grad = (d_kernq * kernel_slope(query_f)).astype(jnp.bfloat16).reshape(out_shape)
    key_grad = (d_kernk * kernel_slope(key_f)).astype(jnp.bfloat16).reshape(out_shape)
    value_grad = d_value.astype(jnp.bfloat16).reshape(out_shape)
    tok_total = lax.psum(local_gate, "tok")
    gate_grad = lax.psum_scatter(tok_total, "img", scatter_dimension=0, tiled=True)
    return (query_grad, key_grad, value_grad, gate_grad, weight_grad)


def solution(mesh):
    in_specs = (
        P(None, "img", "tok", None),
        P(None, "img", "tok", None),
        P(None, "img", "tok", None),
        P(None, "img", "tok", None),
        P("tok", "img"),
        P(),
        P(None, "img", None),
    )
    out_specs = (
        P(None, "img", "tok", None),
        P(None, "img", "tok", None),
        P(None, "img", "tok", None),
        P("img"),
        P("tok", "img"),
    )
    return jax.shard_map(
        on_device, mesh=mesh, in_specs=in_specs, out_specs=out_specs, check_vma=False
    )
```

profile of v0, /device:TPU:1, one launch (start us, length us, event | category | flops | bytes accessed | tf_op | source)
XLA Modules:
  0.0 822.2 jit_solution(7026834833629563472)
XLA Ops:
  7.3 44.5 %all-gather = bf16[32,35,72]{2,1,0:T(8,128)(2,1)S(1)} all-gather(bf16[1,35,72]{2,1,0:T(8,128)(2,1)} %bitcast.135), channel_id=1, replica_groups=mesh['tok'=32,'img'=16] {'tok'}, dimensions={0}, use_global_device_ids=true | all-gather | bytes 166320 | tf_op jit(solution)/shard_map/all_gather | solution.py:24
  54.4 112.4 %all-reduce.5 = (f32[1,10,112]{2,1,0:T(8,128)S(1)}, f32[1,10,112]{2,1,0:T(8,128)S(1)}) all-reduce(f32[1,10,112]{2,1,0:T(8,128)S(1)} %stack.39, f32[1,10,112]{2,1,0:T(8,128)S(1)} %stack.40), channel_id=1, replica_groups=mesh['tok'=32,'img'=16] {'tok'}, use_global_device_ids=true, to_apply=%region_3.4 | all-reduce | flops 2240 | bytes 17920 | tf_op jit(solution)/shard_map/psum | solution.py:37
  169.2 2.3 fusion.36
  171.5 5.3 copy.31
  176.8 2.7 convolution_divide_fusion
  180.6 2.4 fusion.37
  189.5 191.9 %all-reduce.12.cloned.1.call-done = (f32[1,10,112,112]{3,2,1,0:T(8,128)}, f32[1,10,112,112]{3,2,1,0:T(8,128)}, f32[1,10,112,112]{3,2,1,0:T(8,128)}, f32[1,10,112,112]{3,2,1,0:T(8,128)}) async-done(((f32[1,10,112,112]{3,2,1,0:T(8,128)}, f32[1,10,112,112]{3,2,1,0:T(8,128)}, f32[1,10,112,112]{3,2,1,0:T(8,128)}, f32[1,10,112,112]{3,2,1,0:T(8,128)}), (f32[1,10,112,112]{3,2,1,0:T(8,128)}, ...) | async-done | bytes 2007056 | tf_op jit(solution)/shard_map/psum | solution.py:37
  383.0 2.7 fusion.32
  386.5 2.4 convolution_convert_fusion
  388.9 77.8 %fusion = bf16[48,1152]{1,0:T(8,128)(2,1)S(1)} fusion(bf16[1120,1152]{1,0:T(8,128)(2,1)} %convolution_convert_fusion), kind=kCustom, calls=%all-reduce-scatter | all-reduce-scatter fusion | flops 1769473 | bytes 2693120
  467.4 1.9 collective-permute-start.7
  469.3 1.9 collective-permute-start.6
  471.2 1.9 collective-permute-start.5
  473.1 1.9 collective-permute-start.4
  477.2 1.9 fusion.27
  479.2 2.9 fusion.10
  482.1 44.7 %all-reduce = f32[1152]{0:T(1024)S(1)} all-reduce(f32[1152]{0:T(1024)S(1)} %fusion.10), channel_id=2, replica_groups=mesh['tok'=32,'img'=16] {'img'}, use_global_device_ids=true, to_apply=%region_12.13.clone | all-reduce | flops 1152 | bytes 9216
  528.1 4.3 fusion.8
  532.6 114.6 %all-reduce.4 = (f32[1,10,112]{2,1,0:T(8,128)S(1)}, f32[1,10,112]{2,1,0:T(8,128)S(1)}, f32[72]{0:T(128)}) all-reduce(f32[1,10,112]{2,1,0:T(8,128)S(1)} %get-tuple-element.43, f32[1,10,112]{2,1,0:T(8,128)S(1)} %get-tuple-element.42, f32[72]{0:T(128)S(1)} %dynamic-slice.1), channel_id=1, replica_groups=mesh['tok'=32,'img'=16] {'tok'}, use_global_device_ids=true, to_apply=%region_9.10 | all-reduce | flops 2312 | bytes 18496 | tf_op jit(solution)/shard_map/psum | solution.py:68
  652.4 2.9 fusion.9
  655.4 14.6 %concatenate = bf16[451,1152]{1,0:T(8,128)(2,1)} concatenate(bf16[19,1152]{1,0:T(8,128)(2,1)S(1)} %collective-permute-done.8, bf16[48,1152]{1,0:T(8,128)(2,1)} %collective-permute-done.7, bf16[48,1152]{1,0:T(8,128)(2,1)} %collective-permute-done.6, bf16[48,1152]{1,0:T(8,128)(2,1)} %collective-permute-done.5, bf16[48,1152]{1,0:T(8,128)(2,1)} %collective-permute-done.4, ...), dimensions={0} | concatenate | bytes 2078208
  669.9 1.6 dynamic-slice_convert_fusion
  671.6 2.8 convolution_convert_fusion.1
  674.4 139.9 %all-reduce.10.cloned.1.call-done = f32[35,1152]{1,0:T(8,128)} async-done(((f32[35,1152]{1,0:T(8,128)}), f32[35,1152]{1,0:T(8,128)}) %all-reduce.10.cloned.1.call-update) | async-done | bytes 161296
  (92 shorter events, 24.7 us)
Async XLA Ops:
  7.2 162.0 %copy-start = (bf16[2,1,128,1120]{2,3,1,0:T(8,128)(2,1)S(1)}, bf16[2,1,128,1120]{2,3,1,0:T(8,128)(2,1)}, u32[]{:S(2)}) copy-start(bf16[2,1,128,1120]{2,3,1,0:T(8,128)(2,1)} %param.9) | copy-start | bytes 1720324
  7.2 45.6 %copy-start.19 = (f32[2,1,1152]{2,1,0:T(1,128)S(1)}, f32[2,1,1152]{2,1,0:T(1,128)}, u32[]{:S(2)}) copy-start(f32[2,1,1152]{2,1,0:T(1,128)} %param.13) | copy-start | bytes 27652
  7.2 45.6 %copy-start.20 = (f32[1152]{0:T(1024)S(1)}, f32[1152]{0:T(1024)}, u32[]{:S(2)}) copy-start(f32[1152]{0:T(1024)} %param.12) | copy-start | bytes 13828
  7.2 45.6 %copy-start.8 = (bf16[2,1,128,1120]{2,3,1,0:T(8,128)(2,1)S(1)}, bf16[2,1,128,1120]{2,3,1,0:T(8,128)(2,1)}, u32[]{:S(2)}) copy-start(bf16[2,1,128,1120]{2,3,1,0:T(8,128)(2,1)} %param.8) | copy-start | bytes 1720324
  7.2 164.3 %all-gather.3.cloned.1.call-start = ((), (), s32[]{:S(2)}) async-start(), calls=%async_computation | async-start | bytes 2820096 | tf_op jit(solution)/shard_map/all_gather | solution.py:25
  52.7 328.7 %all-reduce.12.cloned.1.call-start = ((), (), s32[]{:S(2)}) async-start(), calls=%async_computation.2 | async-start | bytes 4587520 | tf_op jit(solution)/shard_map/psum | solution.py:37
  52.8 114.0 %copy-start.14 = (bf16[2,1,128,1120]{2,3,1,0:T(8,128)(2,1)S(1)}, bf16[2,1,128,1120]{2,3,1,0:T(8,128)(2,1)}, u32[]{:S(2)}) copy-start(bf16[2,1,128,1120]{2,3,1,0:T(8,128)(2,1)} %param.7) | copy-start | bytes 1720324
  171.5 5.3 copy-start.6
  184.5 629.8 %all-reduce.10.cloned.1.call-start = ((), (), s32[]{:S(2)}) async-start(), calls=%async_computation.1 | async-start | bytes 368640
  388.9 87.4 %copy-start.10 = (f32[1,10,112,112]{3,2,1,0:T(8,128)S(1)}, f32[1,10,112,112]{3,2,1,0:T(8,128)}, u32[]{:S(2)}) copy-start(f32[1,10,112,112]{3,2,1,0:T(8,128)} %get-tuple-element.29) | copy-start | bytes 1505284
  467.4 181.1 %collective-permute-start.7 = (bf16[48,1152]{1,0:T(8,128)(2,1)S(1)}, bf16[48,1152]{1,0:T(8,128)(2,1)}, u32[]{:S(2)}, u32[]{:S(2)}) collective-permute-start(bf16[48,1152]{1,0:T(8,128)(2,1)S(1)} %fusion), channel_id=1, source_target_pairs={{0,128},{16,144},{32,160},{48,176},{64,192},{80,208},{96,224},{112... | collective-permute-start | bytes 331784
  469.3 180.5 %collective-permute-start.6 = (bf16[48,1152]{1,0:T(8,128)(2,1)S(1)}, bf16[48,1152]{1,0:T(8,128)(2,1)}, u32[]{:S(2)}, u32[]{:S(2)}) collective-permute-start(bf16[48,1152]{1,0:T(8,128)(2,1)S(1)} %fusion), channel_id=1, source_target_pairs={{0,112},{16,128},{32,144},{48,160},{64,176},{80,192},{96,208},{112... | collective-permute-start | bytes 331784
  471.2 179.9 %collective-permute-start.5 = (bf16[48,1152]{1,0:T(8,128)(2,1)S(1)}, bf16[48,1152]{1,0:T(8,128)(2,1)}, u32[]{:S(2)}, u32[]{:S(2)}) collective-permute-start(bf16[48,1152]{1,0:T(8,128)(2,1)S(1)} %fusion), channel_id=1, source_target_pairs={{0,96},{16,112},{32,128},{48,144},{64,160},{80,176},{96,192},{112,... | collective-permute-start | bytes 331784
  473.1 182.2 %collective-permute-start.4 = (bf16[48,1152]{1,0:T(8,128)(2,1)S(1)}, bf16[48,1152]{1,0:T(8,128)(2,1)}, u32[]{:S(2)}, u32[]{:S(2)}) collective-permute-start(bf16[48,1152]{1,0:T(8,128)(2,1)S(1)} %fusion), channel_id=1, source_target_pairs={{0,80},{16,96},{32,112},{48,128},{64,144},{80,160},{96,176},{112,1... | collective-permute-start | bytes 331784
  479.2 47.6 %copy-start.18 = (bf16[19,1152]{1,0:T(8,128)(2,1)S(1)}, bf16[19,1152]{1,0:T(8,128)(2,1)}, u32[]{:S(2)}) copy-start(bf16[19,1152]{1,0:T(8,128)(2,1)} %slice.42) | copy-start | bytes 131332
  479.2 48.9 %copy-start.16 = (f32[2,10,112]{2,1,0:T(8,128)S(1)}, f32[2,10,112]{2,1,0:T(8,128)}, u32[]{:S(2)}) copy-start(f32[2,10,112]{2,1,0:T(8,128)} %copy-done.15) | copy-start | bytes 26884
  479.2 48.9 %copy-start.17 = (f32[2,128,10]{1,2,0:T(8,128)S(1)}, f32[2,128,10]{1,2,0:T(8,128)}, u32[]{:S(2)}) copy-start(f32[2,128,10]{1,2,0:T(8,128)} %get-tuple-element.45) | copy-start | bytes 30724
  526.8 120.4 %collective-permute-start.8 = (bf16[19,1152]{1,0:T(8,128)(2,1)S(1)}, bf16[19,1152]{1,0:T(8,128)(2,1)S(1)}, u32[]{:S(2)}, u32[]{:S(2)}) collective-permute-start(bf16[19,1152]{1,0:T(8,128)(2,1)S(1)} %copy-done.18), channel_id=1, source_target_pairs={{0,144},{16,160},{32,176},{48,192},{64,208},{80,224},{96,240},{112... | collective-permute-start | bytes 131336
  528.1 4.3 copy-start.1
  528.1 4.3 copy-start.9
  647.2 8.1 collective-permute-start.3
  648.5 6.8 collective-permute-start.2
  649.8 5.5 collective-permute-start.1
  651.1 4.2 collective-permute-start
  (9 other events, 16.7 us)
Sparse Core Ops, SparseCore 0:
  52.8 51.7 all-gather.2
  184.6 196.7 all-reduce.11
  671.7 142.5 all-reduce.9
where the time goes:
time: 824 us; the launch traced here: 822 us
  blocking collectives  394 us (48%)
  waiting for transfers between devices  332 us (40%)
  local copies, waits for them, and re-layouts  30.2 us (4%)
  matrix products  28.4 us (3%)
  between operations  15.4 us (2%)
  starting transfers between devices  14.3 us (2%)
  other arithmetic  8.25 us (1%)
    psum x1, waiting for transfers between devices, on_device(): lax.psum((state_part[step_idx], keysum_part[step_idx]), 'tok')  192 us
    unnamed x13, waiting for transfers between devices  140 us
    unnamed x2, blocking collectives  122 us
    psum x1, blocking collectives, on_device(): lax.psum((dstate_part[step_idx], dkeysum_part[step_idx]), 'tok')  115 us
    psum x1, blocking collectives, on_device(): lax.psum((state_part[step_idx], keysum_part[step_idx]), 'tok')  112 us
    all_gather x1, blocking collectives, on_device(): row_block = lax.all_gather(out_weight, 'tok', axis=0, tiled=True)  44.5 us
    unnamed x53, local copies, waits for them, and re-layouts  22.7 us
  transfers between devices with their start and end apart: 12, of which 2 were waited for; matrix products, arithmetic and copies ran while one was open for 3% of the time, Pallas kernels for 0%

commit v1 on v0

v1 whole, which is shorter than its diff:
```python
import jax
import jax.numpy as jnp
from jax import lax
from jax.experimental import pallas as pl
from jax.experimental.pallas import tpu as pltpu
from jax.sharding import PartitionSpec as P

HEADS = 10
HEAD = 112
LOSS_SCALE = 1024.0
TOK = 128
F = 1120
DW = 1152
NX, NZ, NY = 4, 8, 8
NT = NX * NZ
LANES = 128
FP = HEADS * LANES
ROWS_T = 35
ROWS_TP = 48
COLS_I = 72
COLS_IP = 80
NG = 2 * NY
DP = NG * COLS_IP
XR = 288
ZR = 48
BF = jnp.bfloat16
F32 = jnp.float32
MESH = pl.DeviceIdType.MESH
NN = (((1,), (0,)), ((), ()))
NTD = (((1,), (1,)), ((), ()))
TN = (((0,), (0,)), ((), ()))


def dot(a, b, dims):
    return lax.dot_general(a, b, dims, preferred_element_type=F32)


def phi(x):
    return jnp.where(x > 0, x + 1.0, jnp.exp(jnp.minimum(x, 0.0)))


def lane_of(shape):
    return lax.broadcasted_iota(jnp.int32, shape, len(shape) - 1)


def row_of(shape):
    return lax.broadcasted_iota(jnp.int32, shape, len(shape) - 2)


def rounded(x):
    return x.astype(BF).astype(F32)


def split_sum(total):
    lane = lane_of(total.shape)
    whole = total[:, HEAD : HEAD + 1] + total[:, HEAD + 1 : HEAD + 2]
    high = rounded(whole)
    out = jnp.where((lane == HEAD) | (lane == HEAD + 2), high, total)
    return jnp.where(lane == HEAD + 1, whole - high, out)


def same(total):
    return total


def loop(first, last, body):
    def step(idx, carry):
        body(idx)
        return carry

    lax.fori_loop(first, last, step, 0)


def kernel(
    q_ref, k_ref, v_ref, cot_ref, w_ref, table_ref, time_ref,
    dq_ref, dk_ref, dv_ref, wg_ref,
    kq, kk, vs, hot_f, hot_d, scaled, sc_rows, sc_cols, cot_cols,
    w_land, w_t, st, d_st, x_src, x_land, z_src, z_land, z_all,
    d_att, att, dna, core_src, core_land, own_band, y_src, y_land, p_src, p_land,
    w_ss, w_rs, wy_ss, wy_rs, wc_ss, wc_rs, ar_ss, ar_rs, c_ss, c_rs, y_ss, y_rs, p_ss, p_rs,
):
    t = lax.axis_index("tok")
    i = lax.axis_index("img")
    x, z = t // NZ, t % NZ
    y, c = i // 2, i % 2
    sib = (t, y * 2 + (1 - c))

    def plane(d):
        return lax.rem(t + d, NT)

    def along_x(d):
        return lax.rem(x + d, NX)

    def along_z(d):
        return lax.rem(z + d, NZ)

    def along_y(d):
        return lax.rem(y + d, NY)

    def remote(src, dst, ss, rs, dev):
        return pltpu.make_async_remote_copy(
            src_ref=src, dst_ref=dst, send_sem=ss, recv_sem=rs, device_id=dev, device_id_type=MESH
        )

    barrier = pltpu.get_barrier_semaphore()

    def greet(dev):
        pl.semaphore_signal(barrier, inc=1, device_id=dev, device_id_type=MESH)

    loop(1, NT, lambda d: greet((plane(d), i)))
    loop(1, NY, lambda d: greet((t, along_y(d) * 2 + c)))
    greet(sib)

    ones = jnp.where(lane_of((2 * TOK, LANES - HEAD)) < 3, 1.0, 0.0).astype(BF)
    none = jnp.zeros((2 * TOK, LANES - HEAD), BF)
    for h in range(HEADS):
        part = slice(HEAD * h, HEAD * h + HEAD)
        kk[h, :, :HEAD] = phi(k_ref[:, part].astype(F32)).astype(BF)
        kk[h, :, HEAD:] = none
        vs[h, :, :HEAD] = v_ref[:, part]
        vs[h, :, HEAD:] = ones

    tail = jnp.zeros((NX * XR - F, LANES), BF)
    for s in range(2):
        for a in range(2):
            x_src[a, s, F:] = tail

    def state_part(s):
        rows = pl.ds(TOK * s, TOK)

        def one(h):
            acc = dot(kk[h, rows, :], vs[h, rows, :], TN)[:HEAD]
            lane = lane_of(acc.shape)
            x_src[0, s, pl.ds(pl.multiple_of(HEAD * h, 16), HEAD), :] = jnp.where(
                lane == HEAD + 1, acc - rounded(acc), acc
            ).astype(BF)

        loop(0, HEADS, one)

    def rs_x(a, s, d):
        to = along_x(d)
        return remote(
            x_src.at[a, s, pl.ds(pl.multiple_of(XR * to, 16), XR)], x_land.at[a, s, d - 1],
            ar_ss.at[a, s, d - 1], ar_rs.at[a, s, d - 1], (to * NZ + z, i),
        )

    def rs_z(a, s, d):
        to = along_z(d)
        return remote(
            z_src.at[a, s, pl.ds(pl.multiple_of(ZR * to, 16), ZR)], z_land.at[a, s, d - 1],
            ar_ss.at[a, s, 2 + d], ar_rs.at[a, s, 2 + d], (x * NZ + to, i),
        )

    def ag_z(a, s, d):
        mine = z_all.at[a, s, pl.ds(pl.multiple_of(ZR * z, 16), ZR)]
        return remote(
            mine, mine, ar_ss.at[a, s, 9 + d], ar_rs.at[a, s, 9 + d], (x * NZ + along_z(d), i)
        )

    def ag_x(a, s, d):
        whole = d_st if a else st
        return remote(
            z_all.at[a, s, pl.ds(0, XR)], whole.at[s, pl.ds(pl.multiple_of(XR * x, 16), XR)],
            ar_ss.at[a, s, 16 + d], ar_rs.at[a, s, 16 + d], (along_x(d) * NZ + z, i),
        )

    def start_x(a, s):
        loop(1, NX, lambda d: rs_x(a, s, d).start())

    def x_to_z(a, s, fix):
        loop(1, NX, lambda d: rs_x(a, s, d).wait_recv())
        total = x_src[a, s, pl.ds(pl.multiple_of(XR * x, 16), XR), :].astype(F32)
        for d in range(NX - 1):
            total = total + x_land[a, s, d].astype(F32)
        z_src[a, s, :XR] = fix(total).astype(BF)
        z_src[a, s, XR:] = jnp.zeros((NZ * ZR - XR, LANES), BF)
        loop(1, NZ, lambda d: rs_z(a, s, d).start())

    def z_to_all(a, s, fix):
        loop(1, NZ, lambda d: rs_z(a, s, d).wait_recv())
        total = z_src[a, s, pl.ds(pl.multiple_of(ZR * z, 16), ZR), :].astype(F32)
        for d in range(NZ - 1):
            total = total + z_land[a, s, d].astype(F32)
        z_all[a, s, pl.ds(pl.multiple_of(ZR * z, 16), ZR), :] = fix(total).astype(BF)
        loop(1, NZ, lambda d: ag_z(a, s, d).start())

    def all_to_x(a, s):
        loop(1, NZ, lambda d: ag_z(a, s, d).wait_recv())
        loop(1, NX, lambda d: ag_x(a, s, d).start())
        whole = d_st if a else st
        whole[s, pl.ds(pl.multiple_of(XR * x, 16), XR), :] = z_all[a, s, :XR]

    def end_x(a, s):
        loop(1, NX, lambda d: ag_x(a, s, d).wait_recv())

    def w_plane(d):
        return remote(w_ref, w_land.at[t], w_ss.at[d - 1], w_rs.at[d - 1], (plane(d), i))

    def group(g):
        return pl.ds(pl.multiple_of(COLS_IP * g, 16), COLS_IP)

    def w_along_y(d):
        mine = w_t.at[group(y * 2 + c)]
        return remote(mine, mine, wy_ss.at[d - 1], wy_rs.at[d - 1], (t, along_y(d) * 2 + c))

    def w_core(d):
        mine = w_t.at[group(along_y(d) * 2 + c)]
        return remote(mine, mine, wc_ss.at[d], wc_rs.at[d], sib)

    state_part(0)
    pl.semaphore_wait(barrier, NT - 1 + NY - 1 + 1)
    loop(1, NT, lambda d: w_plane(d).start())
    start_x(0, 0)
    state_part(1)
    start_x(0, 1)
    w_land[t] = w_ref[...]

    def hot_rows(b):
        shape = (ROWS_TP, FP)
        j, lane = row_of(shape), lane_of(shape)
        f = ROWS_T * b + j
        head = (ROWS_T * b) // HEAD
        at = f + 16 * head + jnp.where(f >= HEAD * (head + 1), 16, 0)
        at = jnp.where(j < ROWS_T, at, jnp.where(j < ROWS_T + 2, HEAD + j - ROWS_T, -1))
        hot_f[pl.ds(pl.multiple_of(ROWS_TP * b, 16), ROWS_TP), :] = jnp.where(lane == at, 1.0, 0.0).astype(BF)

    loop(0, NT, hot_rows)

    def hot_cols(g):
        shape = (COLS_IP, DW)
        j, lane = row_of(shape), lane_of(shape)
        at = jnp.where(j < COLS_I, COLS_I * g + j, -1)
        hot_d[group(g), :] = jnp.where(lane == at, 1.0, 0.0).astype(BF)

    loop(0, NG, hot_cols)

    for s in range(2):
        rows = slice(TOK * s, TOK * s + TOK)
        gate = table_ref[...] + time_ref[s : s + 1, :]
        scaled[rows, :] = ((LOSS_SCALE * gate) * cot_ref[rows, :].astype(F32)).astype(BF)

    x_to_z(0, 0, split_sum)
    x_to_z(0, 1, split_sum)

    def to_groups(b):
        rows = pl.ds(pl.multiple_of(256 * b, 16), 256)
        hot = hot_d[rows, :]
        sc_cols[rows, :] = dot(hot, scaled[...], NTD).astype(BF)
        cot_cols[rows, :] = dot(hot, cot_ref[...], NTD).astype(BF)

    loop(0, DP // 256, to_groups)
    for b in range(DP // 256):
        cols = slice(256 * b, 256 * b + 256)
        sc_rows[:, cols] = dot(scaled[...], hot_d[cols, :], NTD).astype(BF)

    for h in range(HEADS):
        kq[h, :, :HEAD] = phi(q_ref[:, HEAD * h : HEAD * h + HEAD].astype(F32)).astype(BF)
        kq[h, :, HEAD:] = none

    z_to_all(0, 0, split_sum)
    z_to_all(0, 1, split_sum)

    loop(1, NT, lambda d: w_plane(d).wait_recv())
    for b in range(FP // 256):
        cols = slice(256 * b, 256 * b + 256)
        block = dot(w_land[...].reshape(NT * ROWS_TP, LANES), hot_f[:, cols], TN)
        w_t[group(y * 2 + c), cols] = block[:COLS_IP].astype(BF)
    loop(1, NY, lambda d: w_along_y(d).start())
    w_core(0).start()

    all_to_x(0, 0)
    all_to_x(0, 1)

    for d in (1, 7, 2, 6, 3, 5, 4):
        w_along_y(d).wait_recv()
        w_core(NY - d).start()
    loop(0, NY, lambda d: w_core(d).wait_recv())

    for b in range(FP // 256):
        cols = slice(256 * b, 256 * b + 256)
        d_att[:, cols] = dot(sc_rows[...], w_t[:, cols], NN)

    def middle(s):
        rows = pl.ds(TOK * s, TOK)

        for h in range(HEADS):
            cols = slice(LANES * h, LANES * h + LANES)
            e_rows = slice(HEAD * h, HEAD * h + HEAD)
            kq_h = kq[h, rows, :]
            both = dot(kq_h[:, :HEAD], st[s, e_rows, :], NN)
            inv = 1.0 / (both[:, HEAD : HEAD + 1] + both[:, HEAD + 1 : HEAD + 2])
            lane = lane_of(both.shape)
            ratio = jnp.where(lane < HEAD, both * inv, 0.0)
            att[rows, cols] = ratio.astype(BF)
            d_num = rounded(d_att[rows, cols] * inv)
            d_den = -jnp.sum(d_num * ratio, axis=1, keepdims=True)
            high = rounded(d_den)
            full = jnp.where(lane < HEAD, d_num, jnp.where(lane < HEAD + 2, high, 0.0))
            full = jnp.where(lane == HEAD + 2, d_den - high, full).astype(BF)
            dna[h, rows, :] = full
            acc = dot(kq_h, full, TN)[:HEAD]
            x_src[1, s, e_rows, :] = jnp.where(lane_of(acc.shape) == HEAD + 1, 0.0, acc).astype(BF)

    end_x(0, 0)
    middle(0)
    start_x(1, 0)
    end_x(0, 1)
    middle(1)
    start_x(1, 1)

    def band(g):
        block = dot(sc_cols[group(g), :], att[...], NN)
        plain = dot(cot_cols[group(g), :], att[...], NN)
        gate = jnp.sum(plain * w_t[group(g), :].astype(F32), axis=1, keepdims=True)
        high = rounded(gate)
        lane = lane_of(block.shape)
        return jnp.where(lane == HEAD, high, jnp.where(lane == HEAD + 1, gate - high, block))

    def band_core(d):
        return remote(core_src.at[d], core_land.at[d], c_ss.at[d], c_rs.at[d], sib)

    def band_y(d):
        return remote(y_src.at[d], y_land.at[d - 1], y_ss.at[d - 1], y_rs.at[d - 1], (t, along_y(d) * 2 + c))

    def for_sibling(d):
        core_src[d] = band(along_y(d) * 2 + (1 - c)).astype(BF)
        band_core(d).start()

    loop(0, NY, for_sibling)
    x_to_z(1, 0, same)

    def for_self(d):
        own_band[d] = band(along_y(d) * 2 + c)

    loop(0, NY, for_self)
    x_to_z(1, 1, same)

    def add_halves(total):
        lane = lane_of(total.shape)
        whole = total[:, HEAD : HEAD + 1] + total[:, HEAD + 1 : HEAD + 2]
        high = rounded(whole)
        return jnp.where(lane == HEAD, high, jnp.where(lane == HEAD + 1, whole - high, total))

    def to_y(d):
        band_core(d).wait_recv()
        y_src[d] = add_halves(own_band[d] + core_land[d].astype(F32)).astype(BF)

    for d in (4, 3, 5, 2, 6, 1, 7):
        to_y(d)
        band_y(d).start()
    to_y(0)

    z_to_all(1, 0, same)
    z_to_all(1, 1, same)

    def out_heads(ref, s, heads):
        for h in range(HEADS):
            ref[TOK * s : TOK * s + TOK, HEAD * h : HEAD * h + HEAD] = heads(h)[:, :HEAD].astype(BF)

    def dq_head(s):
        rows = slice(TOK * s, TOK * s + TOK)

        def head(h):
            grad = dot(dna[h, rows, :], st[s, HEAD * h : HEAD * h + HEAD, :], NTD)
            return grad * jnp.minimum(kq[h, rows, :HEAD].astype(F32), 1.0)

        return head

    def dk_head(s):
        rows = slice(TOK * s, TOK * s + TOK)

        def head(h):
            grad = dot(vs[h, rows, :], d_st[s, HEAD * h : HEAD * h + HEAD, :], NTD)
            return grad * jnp.minimum(kk[h, rows, :HEAD].astype(F32), 1.0)

        return head

    def dv_head(s):
        rows = slice(TOK * s, TOK * s + TOK)
        return lambda h: dot(kk[h, rows, :HEAD], d_st[s, HEAD * h : HEAD * h + HEAD, :], NN)

    out_heads(dq_ref, 0, dq_head(0))
    out_heads(dq_ref, 1, dq_head(1))
    all_to_x(1, 0)
    all_to_x(1, 1)

    loop(1, NY, lambda d: band_y(d).wait_recv())
    total = y_src[0].astype(F32)
    for d in range(NY - 1):
        total = total + y_land[d].astype(F32)
    total = add_halves(total).astype(BF)
    total = jnp.concatenate([total, jnp.zeros((LANES - COLS_IP, FP), BF)], axis=0)

    def pieces(b):
        rows = pl.ds(pl.multiple_of(ROWS_TP * 4 * b, 16), ROWS_TP * 4)
        p_src[pl.ds(4 * b, 4)] = dot(hot_f[rows, :], total, NTD).astype(BF).reshape(4, ROWS_TP, LANES)

    loop(0, NT // 4, pieces)

    def p_plane(d):
        return remote(p_src.at[plane(d)], p_land.at[d - 1], p_ss.at[d - 1], p_rs.at[d - 1], (plane(d), i))

    loop(1, NT, lambda d: p_plane(d).start())

    for s in range(2):
        end_x(1, s)
        out_heads(dk_ref, s, dk_head(s))
        out_heads(dv_ref, s, dv_head(s))

    loop(1, NT, lambda d: p_plane(d).wait_recv())
    wg_ref[...] = p_src[t].astype(F32) + jnp.sum(p_land[...].astype(F32), axis=0)

    loop(1, NT, lambda d: w_plane(d).wait_send())
    loop(1, NY, lambda d: w_along_y(d).wait_send())
    loop(0, NY, lambda d: w_core(d).wait_send())
    for a in range(2):
        for s in range(2):
            loop(1, NX, lambda d: rs_x(a, s, d).wait_send())
            loop(1, NZ, lambda d: rs_z(a, s, d).wait_send())
            loop(1, NZ, lambda d: ag_z(a, s, d).wait_send())
            loop(1, NX, lambda d: ag_x(a, s, d).wait_send())
    loop(0, NY, lambda d: band_core(d).wait_send())
    loop(1, NY, lambda d: band_y(d).wait_send())
    loop(1, NT, lambda d: p_plane(d).wait_send())


def on_device(query_in, key_in, value_in, cotangent, out_weight, gate_table, time_gate):
    rows = 2 * TOK
    w_pad = jnp.pad(out_weight, ((0, ROWS_TP - ROWS_T), (0, LANES - COLS_I)))
    dma = pltpu.SemaphoreType.DMA
    vm = pltpu.VMEM
    whole = pl.BlockSpec(memory_space=pltpu.VMEM)
    out = pl.pallas_call(
        kernel,
        name="linear_attention_backward",
        out_shape=[jax.ShapeDtypeStruct((rows, F), BF)] * 3 + [jax.ShapeDtypeStruct((ROWS_TP, LANES), F32)],
        in_specs=[whole] * 7,
        out_specs=[whole] * 4,
        scratch_shapes=[
            vm((HEADS, rows, LANES), BF),
            vm((HEADS, rows, LANES), BF),
            vm((HEADS, rows, LANES), BF),
            vm((NT * ROWS_TP, FP), BF),
            vm((DP, DW), BF),
            vm((rows, DW), BF),
            vm((rows, DP), BF),
            vm((DP, rows), BF),
            vm((DP, rows), BF),
            vm((NT, ROWS_TP, LANES), BF),
            vm((DP, FP), BF),
            vm((2, NX * XR, LANES), BF),
            vm((2, NX * XR, LANES), BF),
            vm((2, 2, NX * XR, LANES), BF),
            vm((2, 2, NX - 1, XR, LANES), BF),
            vm((2, 2, NZ * ZR, LANES), BF),
            vm((2, 2, NZ - 1, ZR, LANES), BF),
            vm((2, 2, NZ * ZR, LANES), BF),
            vm((rows, FP), F32),
            vm((rows, FP), BF),
            vm((HEADS, rows, LANES), BF),
            vm((NY, COLS_IP, FP), BF),
            vm((NY, COLS_IP, FP), BF),
            vm((NY, COLS_IP, FP), F32),
            vm((NY, COLS_IP, FP), BF),
            vm((NY - 1, COLS_IP, FP), BF),
            vm((NT, ROWS_TP, LANES), BF),
            vm((NT - 1, ROWS_TP, LANES), BF),
            dma((NT - 1,)), dma((NT - 1,)),
            dma((NY - 1,)), dma((NY - 1,)),
            dma((NY,)), dma((NY,)),
            dma((2, 2, 20)), dma((2, 2, 20)),
            dma((NY,)), dma((NY,)),
            dma((NY - 1,)), dma((NY - 1,)),
            dma((NT - 1,)), dma((NT - 1,)),
        ],
        compiler_params=pltpu.CompilerParams(
            collective_id=0, has_side_effects=True, vmem_limit_bytes=56 * 2**20
        ),
    )(
        query_in.reshape(rows, F),
        key_in.reshape(rows, F),
        value_in.reshape(rows, F),
        cotangent.reshape(rows, DW),
        w_pad,
        gate_table.reshape(1, DW),
        time_gate.reshape(2, DW),
    )
    shape = query_in.shape
    share = out[3]
    return (
        out[0].reshape(shape),
        out[1].reshape(shape),
        out[2].reshape(shape),
        share[ROWS_T, :COLS_I] + share[ROWS_T + 1, :COLS_I],
        share[:ROWS_T, :COLS_I] / LOSS_SCALE,
    )


def solution(mesh):
    big = P(None, "img", "tok", None)
    return jax.shard_map(
        on_device,
        mesh=mesh,
        in_specs=(big, big, big, big, P("tok", "img"), P(), P(None, "img", None)),
        out_specs=(big, big, big, P("img"), P("tok", "img")),
        check_vma=False,
    )
```

time: 824 us -> 159 us (0.19)
  blocking collectives: 394 us -> 0 us
  waiting for transfers between devices: 332 us -> 0 us
  Pallas kernels: 0 us -> 145 us
  matrix products: 28.4 us -> 0 us
  local copies, waits for them, and re-layouts: 30.2 us -> 11.2 us
  between operations: 15.4 us -> 0.67 us
  starting transfers between devices: 14.3 us -> 0 us
    psum x2 -> x0, blocking collectives: 227 us -> none  [the longest x1 115 us: on_device(): lax.psum((dstate_part[step_idx], dkeysum_part[step_idx]), 'tok')]
    psum x1 -> x0, waiting for transfers between devices: 192 us -> none  [on_device(): lax.psum((state_part[step_idx], keysum_part[step_idx]), 'tok')]
    pallas_call x0 -> x1, Pallas kernels: none -> 145 us  [on_device(): pl.pallas_call(kernel, name='linear_attention_backward', out_shape=[jax.S...]
    unnamed x13 -> x0, waiting for transfers between devices: 140 us -> none
    unnamed x2 -> x0, blocking collectives: 122 us -> none
    all_gather x1 -> x0, blocking collectives: 44.5 us -> none  [on_device(): row_block = lax.all_gather(out_weight, 'tok', axis=0, tiled=True)]
    dot_general x11 -> x0, matrix products: 28.4 us -> none  [the longest x1 4.28 us: on_device(): jnp.einsum('sthf,shef->sthe', d_numer, state, precision=highest)]
    unnamed x10 -> x0, starting transfers between devices: 14.2 us -> none
  transfers between devices with their start and end apart: 12 -> 0, of which waited for: 2 -> 0; matrix products, arithmetic and copies ran while one was open for 3% -> 0% of each run, Pallas kernels for 0% -> 0%
where the time goes in v1:
time: 159 us; the launch traced here: 158 us
  Pallas kernels  145 us (91%)
  local copies, waits for them, and re-layouts  11.2 us (7%)
    pallas_call x1, Pallas kernels, on_device(): pl.pallas_call(kernel, name='linear_attention_backward', out_shape=[jax.S...  145 us
    unnamed x21, local copies, waits for them, and re-layouts  9.34 us

profile of v1, /device:TPU:1, one launch (start us, length us, event | category | flops | bytes accessed | tf_op | source)
XLA Modules:
  0.0 158.2 jit_solution(18431234853450246322)
XLA Ops:
  0.6 0.0 copy-start.6
  0.6 1.3 reshape.42.table_ref
  1.9 0.0 copy-done.6
  1.9 0.0 copy-start.5
  1.9 0.6 copy.20
  2.5 0.1 copy-done.5
  2.7 0.6 pad.4.w_ref
  3.3 0.0 copy-start.2
  3.3 2.2 %copy.12 = bf16[2,1,128,1120]{3,2,0,1:T(8,128)(2,1)} copy(bf16[2,1,128,1120]{2,3,1,0:T(8,128)(2,1)} %param.7) | data formatting | bytes 1146880 | tf_op args[0]
  5.4 0.0 copy-done.2
  5.4 0.0 copy-start.3
  5.4 1.1 copy.13
  6.5 0.0 copy-done.3
  6.5 1.1 copy.14
  7.6 145.2 %linear_attention_backward.1 = (bf16[256,1120]{1,0:T(8,128)(2,1)}, bf16[256,1120]{1,0:T(8,128)(2,1)}, bf16[256,1120]{1,0:T(8,128)(2,1)}, f32[48,128]{1,0:T(8,128)}) custom-call(bf16[256,1120]{1,0:T(8,128)(2,1)} %bitcast.12, bf16[256,1120]{1,0:T(8,128)(2,1)} %bitcast.13, bf16[256,1120]{1,0:T(8,128)(2,1)} %bitcast.14, bf16[256,1152]{1,0:T(8,128)(2,1)} %bitcast.18, ...), custom_call_target="tpu_custom_call" | custom-call | tf_op jit(solution)/shard_map/linear_attention_backward/pallas_call | solution.py:433
  152.8 0.0 copy-start.1
  152.8 2.2 %copy.15 = bf16[2,1,128,1120]{2,3,1,0:T(8,128)(2,1)} copy(bf16[2,1,128,1120]{3,2,0,1:T(8,128)(2,1)} %bitcast.17) | data formatting | bytes 1146880
  155.0 0.0 copy-done.1
  155.0 1.1 copy.16
  156.0 0.0 copy-done.4
  156.0 0.5 add_bitcast_fusion
  156.6 0.6 slice_multiply_fusion
  157.2 0.0 copy-done
  157.2 1.1 copy.17
  (2 shorter events, 0.0 us)
Async XLA Ops:
  0.6 1.3 copy-start.6
  1.9 0.7 copy-start.5
  3.3 2.2 %copy-start.2 = (bf16[2,1,128,1120]{2,3,1,0:T(8,128)(2,1)S(1)}, bf16[2,1,128,1120]{2,3,1,0:T(8,128)(2,1)}, u32[]{:S(2)}) copy-start(bf16[2,1,128,1120]{2,3,1,0:T(8,128)(2,1)} %param.8) | copy-start | bytes 1720324
  5.4 1.1 copy-start.3
  152.8 2.2 %copy-start.1 = (bf16[256,1120]{1,0:T(8,128)(2,1)S(1)}, bf16[256,1120]{1,0:T(8,128)(2,1)}, u32[]{:S(2)}) copy-start(bf16[256,1120]{1,0:T(8,128)(2,1)} %get-tuple-element.10) | copy-start | bytes 1720324
  155.0 1.1 copy-start.4
  155.0 2.2 %copy-start = (bf16[256,1120]{1,0:T(8,128)(2,1)S(1)}, bf16[256,1120]{1,0:T(8,128)(2,1)}, u32[]{:S(2)}) copy-start(bf16[256,1120]{1,0:T(8,128)(2,1)} %get-tuple-element.11) | copy-start | bytes 1720324

commit v2 on v0

v2 whole, which is shorter than its diff:
```python
import jax
import jax.numpy as jnp
from jax import lax
from jax.experimental import pallas as pl
from jax.experimental.pallas import tpu as pltpu
from jax.sharding import PartitionSpec as P

HEADS = 10
HEAD = 112
LOSS_SCALE = 1024.0
TOK = 128
F = 1120
DW = 1152
NX, NZ, NY = 4, 8, 8
NT = NX * NZ
LANES = 128
FP = 1152
ROWS_T = 35
ROWS_TP = 48
COLS_I = 72
COLS_IP = 80
HALF = NY * COLS_IP
DP = 2 * HALF
XR = 288
ZR = 48
PART = 48
BF = jnp.bfloat16
F32 = jnp.float32
MESH = pl.DeviceIdType.MESH
NN = (((1,), (0,)), ((), ()))
NTD = (((1,), (1,)), ((), ()))
TN = (((0,), (0,)), ((), ()))


def dot(a, b, dims):
    return lax.dot_general(a, b, dims, preferred_element_type=F32)


def phi(x):
    return jnp.where(x > 0, x + 1.0, jnp.exp(jnp.minimum(x, 0.0)))


def lane_of(shape):
    return lax.broadcasted_iota(jnp.int32, shape, len(shape) - 1)


def row_of(shape):
    return lax.broadcasted_iota(jnp.int32, shape, len(shape) - 2)


def rounded(x):
    return x.astype(BF).astype(F32)


def split_sum(total):
    lane = lane_of(total.shape)
    whole = total[:, HEAD : HEAD + 1] + total[:, HEAD + 1 : HEAD + 2]
    high = rounded(whole)
    out = jnp.where((lane == HEAD) | (lane == HEAD + 2), high, total)
    return jnp.where(lane == HEAD + 1, whole - high, out)


def same(total):
    return total


def loop(first, last, body):
    def step(idx, carry):
        body(idx)
        return carry

    lax.fori_loop(first, last, step, 0)


def kernel(
    q_in, k_in, v_in, cot_in, w_ref, table_ref, time_ref,
    dq_ref, dk_ref, dv_ref, wg_ref, gate_ref,
    kq, kk, vs, hot_f, hot_d, scaled, sc_cols, cot_cols,
    w_mine, w_land, w_t, st, d_st, x_src, x_land, z_src, z_land, z_all,
    d_att, att, inv, dna, core_src, core_land, own_band, y_src, y_land, y_mid, y_far, p_src, p_land,
    g_core, g_core_land, g_src, g_land, cot_ref, q_ref, k_ref, v_ref,
    w_ss, w_rs, wy_ss, wy_rs, wc_ss, wc_rs, ar_ss, ar_rs, c_ss, c_rs, y_ss, y_rs, p_ss, p_rs, g_ss, g_rs, in_sem,
):
    t = lax.axis_index("tok")
    i = lax.axis_index("img")
    x, z = t // NZ, t % NZ
    y, c = i // 2, i % 2
    sib = (t, y * 2 + (1 - c))
    sends, recvs = [], {}

    def plane(d):
        return lax.rem(t + d, NT)

    def along_x(d):
        return lax.rem(x + d, NX)

    def along_z(d):
        return lax.rem(z + d, NZ)

    def along_y(d):
        return lax.rem(y + d, NY)

    def remote(src, dst, ss, rs, dev):
        return pltpu.make_async_remote_copy(
            src_ref=src, dst_ref=dst, send_sem=ss, recv_sem=rs, device_id=dev, device_id_type=MESH
        )

    def launch(make, first, last, key):
        loop(first, last, lambda d: make(d).start())
        sends.append((make, first, last))
        recvs[key] = (make, first, last)

    def arrive(key):
        make, first, last = recvs.pop(key)
        loop(first, last, lambda d: make(d).wait_recv())

    def drain():
        for key in list(recvs):
            arrive(key)
        for make, first, last in sends:
            loop(first, last, lambda d: make(d).wait_send())

    barrier = pltpu.get_barrier_semaphore()

    def greet(dev):
        pl.semaphore_signal(barrier, inc=1, device_id=dev, device_id_type=MESH)

    loads = [
        pltpu.make_async_copy(src, dst, in_sem.at[n])
        for n, (src, dst) in enumerate(((k_in, k_ref), (v_in, v_ref), (cot_in, cot_ref), (q_in, q_ref)))
    ]
    for load in loads:
        load.start()
    loop(1, NT, lambda d: greet((plane(d), i)))
    loop(1, NY, lambda d: greet((t, along_y(d) * 2 + c)))
    greet(sib)

    def group(g):
        return pl.ds(pl.multiple_of(COLS_IP * g, 16), COLS_IP)

    def head_rows(h):
        return pl.ds(pl.multiple_of(HEAD * h, 16), HEAD)

    w_mine[...] = jnp.zeros((ROWS_TP, LANES), BF)
    w_mine[:ROWS_T, :COLS_I] = w_ref[...]
    ones = jnp.where(row_of((LANES - HEAD, TOK)) < 3, 1.0, 0.0).astype(BF)

    def state_part(s):
        for h in range(HEADS):
            rows = slice(HEAD * h, HEAD * h + HEAD)
            keys = phi(k_ref[s, rows, :].astype(F32)).astype(BF)
            kk[s, rows, :] = keys
            vs[s, h, :HEAD, :] = v_ref[s, rows, :]
            vs[s, h, HEAD:, :] = ones
            acc = dot(keys, vs[s, h], NTD)
            x_src[0, s, rows, :] = jnp.where(
                lane_of(acc.shape) == HEAD + 1, acc - rounded(acc), acc
            ).astype(BF)

    def rs_x(a, s):
        def make(d):
            to = along_x(d)
            return remote(
                x_src.at[a, s, pl.ds(pl.multiple_of(XR * to, 16), XR)], x_land.at[a, s, d - 1],
                ar_ss.at[a, s, d - 1], ar_rs.at[a, s, d - 1], (to * NZ + z, i),
            )

        return make

    def rs_z(a, s):
        def make(d):
            to = along_z(d)
            return remote(
                z_src.at[a, s, pl.ds(pl.multiple_of(ZR * to, 16), ZR)], z_land.at[a, s, d - 1],
                ar_ss.at[a, s, 2 + d], ar_rs.at[a, s, 2 + d], (x * NZ + to, i),
            )

        return make

    def ag_z(a, s):
        def make(d):
            mine = z_all.at[a, s, pl.ds(pl.multiple_of(ZR * z, 16), ZR)]
            return remote(
                mine, mine, ar_ss.at[a, s, 9 + d], ar_rs.at[a, s, 9 + d], (x * NZ + along_z(d), i)
            )

        return make

    def ag_x(a, s):
        whole = d_st if a else st

        def make(d):
            return remote(
                z_all.at[a, s, pl.ds(0, XR)], whole.at[s, pl.ds(pl.multiple_of(XR * x, 16), XR)],
                ar_ss.at[a, s, 16 + d], ar_rs.at[a, s, 16 + d], (along_x(d) * NZ + z, i),
            )

        return make

    def start_x(a, s):
        launch(rs_x(a, s), 1, NX, ("rx", a, s))

    def x_to_z(a, s, fix):
        arrive(("rx", a, s))
        total = x_src[a, s, pl.ds(pl.multiple_of(XR * x, 16), XR), :].astype(F32)
        for d in range(NX - 1):
            total = total + x_land[a, s, d].astype(F32)
        z_src[a, s, :XR] = fix(total).astype(BF)
        launch(rs_z(a, s), 1, NZ, ("rz", a, s))

    def z_to_all(a, s, fix):
        arrive(("rz", a, s))
        total = z_src[a, s, pl.ds(pl.multiple_of(ZR * z, 16), ZR), :].astype(F32)
        for d in range(NZ - 1):
            total = total + z_land[a, s, d].astype(F32)
        z_all[a, s, pl.ds(pl.multiple_of(ZR * z, 16), ZR), :] = fix(total).astype(BF)
        launch(ag_z(a, s), 1, NZ, ("az", a, s))

    def all_to_x(a, s):
        arrive(("az", a, s))
        launch(ag_x(a, s), 1, NX, ("ax", a, s))
        whole = d_st if a else st
        whole[s, pl.ds(pl.multiple_of(XR * x, 16), XR), :] = z_all[a, s, :XR]

    def w_plane(d):
        return remote(w_mine, w_land.at[t], w_ss.at[d - 1], w_rs.at[d - 1], (plane(d), i))

    def tree(which):
        def make(ss, rs, src, dst, step):
            return remote(src, dst, ss.at[which], rs.at[which], (t, along_y(step) * 2 + c))

        return make

    def w_rows(away, first=0, count=COLS_IP):
        return w_t.at[pl.ds(pl.multiple_of(COLS_IP * (c * NY + along_y(away)) + first, 16), count)]

    def w_near(which):
        part = w_rows(0)
        return tree(which)(wy_ss, wy_rs, part, part, (1, 7, 2, 6)[which])

    def w_far(which):
        part = w_rows((6, 2)[which])
        return tree(4 + which)(wy_ss, wy_rs, part, part, (1, 7)[which])

    def w_half(which):
        part = (w_rows(6, PART, COLS_IP - PART), w_rows(2, 0, PART))[which]
        return tree(6 + which)(wy_ss, wy_rs, part, part, (2, 6)[which])

    def w_core(d):
        mine = w_t.at[group(c * NY + along_y(d))]
        return remote(mine, mine, wc_ss.at[d], wc_rs.at[d], sib)

    def band_core(d):
        return remote(core_src.at[d], core_land.at[d], c_ss.at[d], c_rs.at[d], sib)

    def b_tree(n):
        ahead, behind = along_y(4), along_y(4)
        src, dst, step = (
            lambda: (y_src.at[along_y(1)], y_land.at[0], 1),
            lambda: (y_src.at[along_y(7)], y_land.at[1], 7),
            lambda: (y_mid.at[0], y_land.at[2], 2),
            lambda: (y_mid.at[1], y_land.at[3], 6),
            lambda: (y_src.at[along_y(3)], y_far.at[0], 1),
            lambda: (y_src.at[along_y(5)], y_far.at[1], 7),
            lambda: (y_src.at[ahead, pl.ds(0, PART)], y_far.at[2, pl.ds(0, PART)], 2),
            lambda: (y_src.at[behind, pl.ds(PART, COLS_IP - PART)], y_far.at[2, pl.ds(PART, COLS_IP - PART)], 6),
        )[n]()
        return tree(n)(y_ss, y_rs, src, dst, step)

    def gate_core():
        return remote(g_core, g_core_land, g_ss.at[0], g_rs.at[0], sib)

    def gate_y(d):
        return remote(g_src.at[group(along_y(d))], g_land.at[d - 1], g_ss.at[d], g_rs.at[d], (t, along_y(d) * 2 + c))

    def halves(column):
        high = rounded(column)
        lane = lane_of((column.shape[0], LANES)) + (FP - LANES)
        return jnp.where(lane == F, high, jnp.where(lane == F + 1, column - high, 0.0))

    def add_halves(tile):
        at = F - FP + LANES
        return halves(tile[:, at : at + 1] + tile[:, at + 1 : at + 2])

    def main():
        for a in range(2):
            for s in range(2):
                x_src[a, s, F:] = jnp.zeros((NX * XR - F, LANES), BF)
                z_src[a, s, XR:] = jnp.zeros((NZ * ZR - XR, LANES), BF)
        att[F:, :] = jnp.zeros((FP - F, 2 * TOK), BF)
        pl.semaphore_wait(barrier, NT - 1 + NY - 1 + 1)
        launch(w_plane, 1, NT, "w")
        loads[0].wait()
        loads[1].wait()
        state_part(0)
        start_x(0, 0)
        state_part(1)
        start_x(0, 1)
        w_land[t] = w_mine[...]

        def hot_rows(b):
            shape = (ROWS_TP, FP)
            j, lane = row_of(shape), lane_of(shape)
            at = jnp.where(j < ROWS_T, ROWS_T * b + j, jnp.where(j < ROWS_T + 2, F - ROWS_T + j, -1))
            hot_f[pl.ds(pl.multiple_of(ROWS_TP * b, 16), ROWS_TP), :] = jnp.where(lane == at, 1.0, 0.0).astype(BF)

        loop(0, NT, hot_rows)
        x_to_z(0, 0, split_sum)
        x_to_z(0, 1, split_sum)

        def hot_cols(g):
            shape = (COLS_IP, DW)
            j, lane = row_of(shape), lane_of(shape)
            first = COLS_I * (2 * (g % NY) + g // NY)
            hot_d[group(g), :] = jnp.where(lane == jnp.where(j < COLS_I, first + j, -1), 1.0, 0.0).astype(BF)

        loop(0, 2 * NY, hot_cols)
        loads[2].wait()
        loads[3].wait()
        for s in range(2):
            rows = slice(TOK * s, TOK * s + TOK)
            gate = table_ref[...].reshape(1, DW) + time_ref[s]
            scaled[rows, :] = ((LOSS_SCALE * gate) * cot_ref[rows, :].astype(F32)).astype(BF)

        def to_groups(b):
            rows = pl.ds(pl.multiple_of(256 * b, 16), 256)
            hot = hot_d[rows, :]
            sc_cols[rows, :] = dot(hot, scaled[...], NTD).astype(BF)
            cot_cols[rows, :] = dot(hot, cot_ref[...], NTD).astype(BF)

        loop(0, DP // 256, to_groups)
        for s in range(2):
            for h in range(HEADS):
                rows = slice(HEAD * h, HEAD * h + HEAD)
                kq[s, rows, :] = phi(q_ref[s, rows, :].astype(F32)).astype(BF)

        z_to_all(0, 0, split_sum)
        z_to_all(0, 1, split_sum)

        arrive("w")
        for b in range(FP // 384):
            cols = slice(384 * b, 384 * b + 384)
            block = dot(w_land[...].reshape(NT * ROWS_TP, LANES), hot_f[:, cols], TN)
            w_t[group(c * NY + y), cols] = block[:COLS_IP].astype(BF)
        for n in range(4):
            w_near(n).start()
        w_core(0).start()

        all_to_x(0, 0)
        all_to_x(0, 1)

        def ratios(s):
            cols = slice(TOK * s, TOK * s + TOK)
            for h in range(HEADS):
                rows = slice(HEAD * h, HEAD * h + HEAD)
                both = dot(st[s, rows, :], kq[s, rows, :], TN)
                one_over = 1.0 / (both[HEAD : HEAD + 1] + both[HEAD + 1 : HEAD + 2])
                inv[s, h] = one_over
                att[rows, cols] = (both[:HEAD] * one_over).astype(BF)

        arrive(("ax", 0, 0))
        ratios(0)
        w_near(2).wait_recv()
        w_far(0).start()
        w_half(0).start()
        w_core(6).start()
        w_near(3).wait_recv()
        w_far(1).start()
        w_half(1).start()
        w_core(2).start()
        w_near(0).wait_recv()
        w_core(7).start()
        w_near(1).wait_recv()
        w_core(1).start()
        arrive(("ax", 0, 1))
        ratios(1)

        def band(first):
            rows = pl.ds(pl.multiple_of(first, 16), 2 * COLS_IP)
            return dot(sc_cols[rows, :], att[...], NTD)

        for b in range(NY // 2):
            block = band(HALF * (1 - c) + 2 * COLS_IP * b)
            for e in range(2):
                core_src[2 * b + e] = block[COLS_IP * e : COLS_IP * (e + 1)].astype(BF)
            loop(2 * b, 2 * b + 2, lambda d: band_core(d).start())
        for b in range(NY // 2):
            block = band(HALF * c + 2 * COLS_IP * b)
            for e in range(2):
                own_band[2 * b + e] = block[COLS_IP * e : COLS_IP * (e + 1)]
        loop(0, NY, lambda d: band_core(d).wait_recv())

        def to_y(d):
            y_src[d] = (own_band[d] + core_land[d].astype(F32)).astype(BF)

        loop(0, NY, to_y)
        for n in (4, 5, 6, 7, 0, 1):
            b_tree(n).start()
        w_far(0).wait_recv()
        w_core(5).start()
        w_far(1).wait_recv()
        w_core(3).start()
        w_half(0).wait_recv()
        w_half(1).wait_recv()
        w_core(4).start()
        loop(0, NY, lambda d: w_core(d).wait_recv())

        for b in range(FP // 384):
            cols = slice(384 * b, 384 * b + 384)
            d_att[cols, :] = dot(w_t[:, cols], sc_cols[...], TN)

        def middle(s):
            cols = slice(TOK * s, TOK * s + TOK)
            for h in range(HEADS):
                rows = slice(HEAD * h, HEAD * h + HEAD)
                d_num = rounded(d_att[rows, cols] * inv[s, h])
                d_den = -jnp.sum(d_num * att[rows, cols].astype(F32), axis=0, keepdims=True)
                high = rounded(d_den)
                row = row_of((LANES - HEAD, TOK))
                rest = jnp.where(row < 2, high, jnp.where(row == 2, d_den - high, 0.0))
                dna[s, h, :HEAD] = d_num.astype(BF)
                dna[s, h, HEAD:] = rest.astype(BF)
                acc = dot(kq[s, rows, :], dna[s, h], NTD)
                x_src[1, s, rows, :] = jnp.where(lane_of(acc.shape) == HEAD + 1, 0.0, acc).astype(BF)

        middle(0)
        start_x(1, 0)
        middle(1)
        start_x(1, 1)

        def gate_tile(first):
            rows = pl.ds(pl.multiple_of(first, 16), HALF // 2)
            part = dot(w_t[rows, :], att[...], NN) * cot_cols[rows, :].astype(F32)
            return halves(jnp.sum(part, axis=1, keepdims=True))

        for b in range(2):
            rows = slice(HALF // 2 * b, HALF // 2 * (b + 1))
            g_core[rows, :] = gate_tile(HALF * (1 - c) + HALF // 2 * b).astype(BF)
        gate_core().start()
        x_to_z(1, 0, same)
        x_to_z(1, 1, same)
        gate_core().wait_recv()
        for b in range(2):
            rows = slice(HALF // 2 * b, HALF // 2 * (b + 1))
            part = gate_tile(HALF * c + HALF // 2 * b) + g_core_land[rows, :].astype(F32)
            g_src[rows, :] = add_halves(part).astype(BF)
        launch(gate_y, 1, NY, "g")

        b_tree(4).wait_recv()
        b_tree(6).wait_recv()
        to = along_y(2)
        y_mid[0] = (y_src[to].astype(F32) + y_far[0].astype(F32)).astype(BF)
        y_mid[0, :PART] = (
            y_src[to, :PART].astype(F32) + y_far[0, :PART].astype(F32) + y_far[2, :PART].astype(F32)
        ).astype(BF)
        b_tree(2).start()
        b_tree(5).wait_recv()
        b_tree(7).wait_recv()
        to = along_y(6)
        y_mid[1] = (y_src[to].astype(F32) + y_far[1].astype(F32)).astype(BF)
        y_mid[1, PART:] = (
            y_src[to, PART:].astype(F32) + y_far[1, PART:].astype(F32) + y_far[2, PART:].astype(F32)
        ).astype(BF)
        b_tree(3).start()

        z_to_all(1, 0, same)
        z_to_all(1, 1, same)

        for s in range(2):
            for h in range(HEADS):
                rows = slice(HEAD * h, HEAD * h + HEAD)
                grad = dot(st[s, rows, :], dna[s, h], NN)
                slope = jnp.minimum(kq[s, rows, :].astype(F32), 1.0)
                dq_ref[s, rows, :] = (grad * slope).astype(BF)
        all_to_x(1, 0)
        all_to_x(1, 1)

        def last_grads(s):
            arrive(("ax", 1, s))
            for h in range(HEADS):
                rows = slice(HEAD * h, HEAD * h + HEAD)
                keys = kk[s, rows, :]
                state = d_st[s, rows, :]
                grad = dot(state, vs[s, h], NN)
                dk_ref[s, rows, :] = (grad * jnp.minimum(keys.astype(F32), 1.0)).astype(BF)
                dv_ref[s, rows, :] = dot(state, keys, TN)[:HEAD].astype(BF)

        last_grads(0)
        last_grads(1)

        for n in range(4):
            b_tree(n).wait_recv()
        total = y_src[y].astype(F32)
        for d in range(4):
            total = total + y_land[d].astype(F32)
        arrive("g")
        gate = g_src[group(y), :].astype(F32)
        for d in range(NY - 1):
            gate = gate + g_land[d].astype(F32)
        last = total[:, FP - LANES :] + add_halves(gate)
        total = jnp.concatenate([total[:, : FP - LANES], last], axis=1).astype(BF)
        total = jnp.concatenate([total, jnp.zeros((LANES - COLS_IP, FP), BF)], axis=0)

        def pieces(b):
            rows = pl.ds(pl.multiple_of(ROWS_TP * 8 * b, 16), ROWS_TP * 8)
            p_src[pl.ds(8 * b, 8)] = dot(hot_f[rows, :], total, NTD).astype(BF).reshape(8, ROWS_TP, LANES)

        loop(0, NT // 8, pieces)

        def p_plane(d):
            return remote(p_src.at[plane(d)], p_land.at[d - 1], p_ss.at[d - 1], p_rs.at[d - 1], (plane(d), i))

        launch(p_plane, 1, NT, "p")
        arrive("p")
        total = p_src[t].astype(F32)
        for d in range(NT - 1):
            total = total + p_land[d].astype(F32)
        wg_ref[...] = total[:ROWS_T, :COLS_I] * (1.0 / LOSS_SCALE)
        gate_ref[...] = total[ROWS_T : ROWS_T + 1, :COLS_I] + total[ROWS_T + 1 : ROWS_T + 2, :COLS_I]

    main()
    drain()
    for n in range(4):
        w_near(n).wait_send()
    for n in range(2):
        w_far(n).wait_send()
        w_half(n).wait_send()
    loop(0, NY, lambda d: w_core(d).wait_send())
    loop(0, NY, lambda d: band_core(d).wait_send())
    for n in range(8):
        b_tree(n).wait_send()
    gate_core().wait_send()


def on_device(query_in, key_in, value_in, cotangent, out_weight, gate_table, time_gate):
    dma = pltpu.SemaphoreType.DMA
    vm = pltpu.VMEM
    whole = pl.BlockSpec(memory_space=pltpu.VMEM)
    turned = lambda a: jnp.swapaxes(a, 2, 3).reshape(2, F, TOK)
    out = pl.pallas_call(
        kernel,
        name="linear_attention_backward",
        out_shape=[jax.ShapeDtypeStruct((2, F, TOK), BF)] * 3
        + [jax.ShapeDtypeStruct((ROWS_T, COLS_I), F32), jax.ShapeDtypeStruct((1, COLS_I), F32)],
        in_specs=[pl.BlockSpec(memory_space=pl.ANY)] * 4 + [whole] * 3,
        out_specs=[whole] * 5,
        scratch_shapes=[
            vm((2, F, TOK), BF),
            vm((2, F, TOK), BF),
            vm((2, HEADS, LANES, TOK), BF),
            vm((NT * ROWS_TP, FP), BF),
            vm((DP, DW), BF),
            vm((2 * TOK, DW), BF),
            vm((DP, 2 * TOK), BF),
            vm((DP, 2 * TOK), BF),
            vm((ROWS_TP, LANES), BF),
            vm((NT, ROWS_TP, LANES), BF),
            vm((DP, FP), BF),
            vm((2, NX * XR, LANES), BF),
            vm((2, NX * XR, LANES), BF),
            vm((2, 2, NX * XR, LANES), BF),
            vm((2, 2, NX - 1, XR, LANES), BF),
            vm((2, 2, NZ * ZR, LANES), BF),
            vm((2, 2, NZ - 1, ZR, LANES), BF),
            vm((2, 2, NZ * ZR, LANES), BF),
            vm((FP, 2 * TOK), F32),
            vm((FP, 2 * TOK), BF),
            vm((2, HEADS, 1, TOK), F32),
            vm((2, HEADS, LANES, TOK), BF),
            vm((NY, COLS_IP, FP), BF),
            vm((NY, COLS_IP, FP), BF),
            vm((NY, COLS_IP, FP), F32),
            vm((NY, COLS_IP, FP), BF),
            vm((4, COLS_IP, FP), BF),
            vm((2, COLS_IP, FP), BF),
            vm((3, COLS_IP, FP), BF),
            vm((NT, ROWS_TP, LANES), BF),
            vm((NT - 1, ROWS_TP, LANES), BF),
            vm((HALF, LANES), BF),
            vm((HALF, LANES), BF),
            vm((HALF, LANES), BF),
            vm((NY - 1, COLS_IP, LANES), BF),
            vm((2 * TOK, DW), BF),
            vm((2, F, TOK), BF),
            vm((2, F, TOK), BF),
            vm((2, F, TOK), BF),
            dma((NT - 1,)), dma((NT - 1,)),
            dma((8,)), dma((8,)),
            dma((NY,)), dma((NY,)),
            dma((2, 2, 20)), dma((2, 2, 20)),
            dma((NY,)), dma((NY,)),
            dma((8,)), dma((8,)),
            dma((NT - 1,)), dma((NT - 1,)),
            dma((NY,)), dma((NY,)), dma((4,)),
        ],
        compiler_params=pltpu.CompilerParams(
            collective_id=0, has_side_effects=True, vmem_limit_bytes=56 * 2**20
        ),
    )(
        turned(query_in),
        turned(key_in),
        turned(value_in),
        cotangent.reshape(2 * TOK, DW),
        out_weight,
        gate_table,
        time_gate,
    )
    back = lambda a: jnp.swapaxes(a.reshape(2, 1, F, TOK), 2, 3)
    return back(out[0]), back(out[1]), back(out[2]), out[4].reshape(COLS_I), out[3]


def solution(mesh):
    big = P(None, "img", "tok", None)
    return jax.shard_map(
        on_device,
        mesh=mesh,
        in_specs=(big, big, big, big, P("tok", "img"), P(), P(None, "img", None)),
        out_specs=(big, big, big, P("img"), P("tok", "img")),
        check_vma=False,
    )
```

time: 824 us -> 113 us (0.14)
  blocking collectives: 394 us -> 0 us
  waiting for transfers between devices: 332 us -> 0 us
  Pallas kernels: 0 us -> 107 us
  matrix products: 28.4 us -> 0 us
  local copies, waits for them, and re-layouts: 30.2 us -> 5.17 us
  between operations: 15.4 us -> 0.66 us
  starting transfers between devices: 14.3 us -> 0 us
  other arithmetic: 8.25 us -> 0 us
    psum x2 -> x0, blocking collectives: 227 us -> none  [the longest x1 115 us: on_device(): lax.psum((dstate_part[step_idx], dkeysum_part[step_idx]), 'tok')]
    psum x1 -> x0, waiting for transfers between devices: 192 us -> none  [on_device(): lax.psum((state_part[step_idx], keysum_part[step_idx]), 'tok')]
    unnamed x13 -> x0, waiting for transfers between devices: 140 us -> none
    unnamed x2 -> x0, blocking collectives: 122 us -> none
    pallas_call x0 -> x1, Pallas kernels: none -> 107 us  [on_device(): pl.pallas_call(kernel, name='linear_attention_backward', out_shape=[jax.S...]
    all_gather x1 -> x0, blocking collectives: 44.5 us -> none  [on_device(): row_block = lax.all_gather(out_weight, 'tok', axis=0, tiled=True)]
    dot_general x11 -> x0, matrix products: 28.4 us -> none  [the longest x1 4.28 us: on_device(): jnp.einsum('sthf,shef->sthe', d_numer, state, precision=highest)]
    unnamed x53 -> x13, local copies, waits for them, and re-layouts: 22.7 us -> 5.17 us
  transfers between devices with their start and end apart: 12 -> 0, of which waited for: 2 -> 0; matrix products, arithmetic and copies ran while one was open for 3% -> 0% of each run, Pallas kernels for 0% -> 0%
where the time goes in v2:
time: 113 us
  Pallas kernels  107 us (95%)
  local copies, waits for them, and re-layouts  5.17 us (5%)
    pallas_call x1, Pallas kernels, on_device(): pl.pallas_call(kernel, name='linear_attention_backward', out_shape=[jax.S...  107 us
    unnamed x13, local copies, waits for them, and re-layouts  5.17 us

profile of v2, /device:TPU:1, one launch (start us, length us, event | category | flops | bytes accessed | tf_op | source)
XLA Modules:
  0.0 113.0 jit_solution(2463565555702849924)
XLA Ops:
  0.6 107.2 %linear_attention_backward.1 = (bf16[2,1120,128]{2,1,0:T(8,128)(2,1)}, bf16[2,1120,128]{2,1,0:T(8,128)(2,1)}, bf16[2,1120,128]{2,1,0:T(8,128)(2,1)}, f32[35,72]{1,0:T(8,128)}, f32[1,72]{1,0:T(1,128)}) custom-call(bf16[2,1120,128]{2,1,0:T(8,128)(2,1)} %bitcast.33, bf16[2,1120,128]{2,1,0:T(8,128)(2,1)} %bitcast.34, bf16[2,1120,128]{2,1,0:T(8,128)(2,1)} %bitcast.35, ...), custom_call_target="tpu_custom_call" | custom-call | tf_op jit(solution)/shard_map/linear_attention_backward/pallas_call | solution.py:540
  107.8 0.0 copy-start.1
  107.8 2.0 %copy.23 = bf16[2,1,128,1120]{2,3,1,0:T(8,128)(2,1)} copy(bf16[2,1,128,1120]{2,3,1,0:T(8,128)(2,1)} %bitcast.38) | data formatting | bytes 1146880
  109.8 0.0 copy-done.1
  109.8 0.0 copy-start
  109.8 0.8 copy.24
  110.6 0.5 copy-done
  111.1 0.0 copy-start.3
  111.1 0.0 copy-start.2
  111.1 0.8 copy.25
  111.9 0.0 copy-done.3
  111.9 0.5 copy.26
  112.4 0.0 copy-done.2
  112.4 0.6 copy.27
Async XLA Ops:
  107.8 2.0 %copy-start.1 = (bf16[2,1120,128]{2,1,0:T(8,128)(2,1)S(1)}, bf16[2,1120,128]{2,1,0:T(8,128)(2,1)}, u32[]{:S(2)}) copy-start(bf16[2,1120,128]{2,1,0:T(8,128)(2,1)} %get-tuple-element.11) | copy-start | bytes 1720324
  109.8 1.3 %copy-start = (bf16[2,1120,128]{2,1,0:T(8,128)(2,1)S(1)}, bf16[2,1120,128]{2,1,0:T(8,128)(2,1)}, u32[]{:S(2)}) copy-start(bf16[2,1120,128]{2,1,0:T(8,128)(2,1)} %get-tuple-element.12) | copy-start | bytes 1720324
  111.1 0.8 copy-start.3
  111.1 1.3 %copy-start.2 = (f32[35,72]{1,0:T(8,128)S(1)}, f32[35,72]{1,0:T(8,128)}, u32[]{:S(2)}) copy-start(f32[35,72]{1,0:T(8,128)} %get-tuple-element.29) | copy-start | bytes 30244

commit v3 on v2

v3 whole, which is shorter than its diff:
```python
import jax
import jax.numpy as jnp
from jax import lax
from jax.experimental import pallas as pl
from jax.experimental.pallas import tpu as pltpu
from jax.sharding import PartitionSpec as P

HEADS = 10
HEAD = 112
LOSS_SCALE = 1024.0
TOK = 128
F = 1120
DW = 1152
NX, NZ, NY = 4, 8, 8
NT = NX * NZ
LANES = 128
FP = 1152
ROWS_T = 35
ROWS_TP = 48
COLS_I = 72
COLS_IP = 80
HALF = NY * COLS_IP
DP = 2 * HALF
XR = 288
ZR = 48
PART = 48
BF = jnp.bfloat16
F32 = jnp.float32
MESH = pl.DeviceIdType.MESH
NN = (((1,), (0,)), ((), ()))
NTD = (((1,), (1,)), ((), ()))
TN = (((0,), (0,)), ((), ()))


def dot(a, b, dims):
    return lax.dot_general(a, b, dims, preferred_element_type=F32)


def phi(x):
    return jnp.where(x > 0, x + 1.0, jnp.exp(jnp.minimum(x, 0.0)))


def lane_of(shape):
    return lax.broadcasted_iota(jnp.int32, shape, len(shape) - 1)


def row_of(shape):
    return lax.broadcasted_iota(jnp.int32, shape, len(shape) - 2)


def rounded(x):
    return x.astype(BF).astype(F32)


def split_sum(total):
    lane = lane_of(total.shape)
    whole = total[:, HEAD : HEAD + 1] + total[:, HEAD + 1 : HEAD + 2]
    high = rounded(whole)
    out = jnp.where((lane == HEAD) | (lane == HEAD + 2), high, total)
    return jnp.where(lane == HEAD + 1, whole - high, out)


def same(total):
    return total


def loop(first, last, body):
    def step(idx, carry):
        body(idx)
        return carry

    lax.fori_loop(first, last, step, 0)


def kernel(
    q_in, k_in, v_in, cot_in, w_ref, table_ref, time_ref,
    dq_ref, dk_ref, dv_ref, wg_ref, gate_ref,
    kq, kk, vs, hot_f, hot_d, scaled, sc_cols, cot_cols,
    w_mine, w_land, w_t, st, d_st, x_src, x_land, z_src, z_land, z_all,
    d_att, att, inv, dna, core_src, core_land, own_band, y_src, y_land, y_mid, y_far, p_sum, p_src, p_land,
    g_core, g_core_land, g_src, g_land, cot_ref, q_ref, k_ref, v_ref,
    w_ss, w_rs, wy_ss, wy_rs, wc_ss, wc_rs, ar_ss, ar_rs, c_ss, c_rs, y_ss, y_rs, p_ss, p_rs, g_ss, g_rs, in_sem,
):
    t = lax.axis_index("tok")
    i = lax.axis_index("img")
    x, z = t // NZ, t % NZ
    y, c = i // 2, i % 2
    sib = (t, y * 2 + (1 - c))
    sends, recvs = [], {}

    def plane(d):
        return lax.rem(t + d, NT)

    def along_x(d):
        return lax.rem(x + d, NX)

    def along_z(d):
        return lax.rem(z + d, NZ)

    def along_y(d):
        return lax.rem(y + d, NY)

    def remote(src, dst, ss, rs, dev):
        return pltpu.make_async_remote_copy(
            src_ref=src, dst_ref=dst, send_sem=ss, recv_sem=rs, device_id=dev, device_id_type=MESH
        )

    def launch(make, first, last, key):
        loop(first, last, lambda d: make(d).start())
        sends.append((make, first, last))
        recvs[key] = (make, first, last)

    def arrive(key):
        make, first, last = recvs.pop(key)
        loop(first, last, lambda d: make(d).wait_recv())

    def drain():
        for key in list(recvs):
            arrive(key)
        for make, first, last in sends:
            loop(first, last, lambda d: make(d).wait_send())

    barrier = pltpu.get_barrier_semaphore()

    def greet(dev):
        pl.semaphore_signal(barrier, inc=1, device_id=dev, device_id_type=MESH)

    loads = [
        pltpu.make_async_copy(src, dst, in_sem.at[n])
        for n, (src, dst) in enumerate(((k_in, k_ref), (v_in, v_ref), (cot_in, cot_ref), (q_in, q_ref)))
    ]
    for load in loads:
        load.start()
    loop(1, NT, lambda d: greet((plane(d), i)))
    loop(1, NY, lambda d: greet((t, along_y(d) * 2 + c)))
    greet(sib)

    def group(g):
        return pl.ds(pl.multiple_of(COLS_IP * g, 16), COLS_IP)

    def head_rows(h):
        return pl.ds(pl.multiple_of(HEAD * h, 16), HEAD)

    w_mine[...] = jnp.zeros((ROWS_TP, LANES), BF)
    w_mine[:ROWS_T, :COLS_I] = w_ref[...]
    ones = jnp.where(row_of((LANES - HEAD, TOK)) < 3, 1.0, 0.0).astype(BF)

    def state_part(s):
        for h in range(HEADS):
            rows = slice(HEAD * h, HEAD * h + HEAD)
            keys = phi(k_ref[s, rows, :].astype(F32)).astype(BF)
            kk[s, rows, :] = keys
            vs[s, h, :HEAD, :] = v_ref[s, rows, :]
            vs[s, h, HEAD:, :] = ones
            acc = dot(keys, vs[s, h], NTD)
            x_src[0, s, rows, :] = jnp.where(
                lane_of(acc.shape) == HEAD + 1, acc - rounded(acc), acc
            ).astype(BF)

    def rs_x(a, s):
        def make(d):
            to = along_x(d)
            return remote(
                x_src.at[a, s, pl.ds(pl.multiple_of(XR * to, 16), XR)], x_land.at[a, s, d - 1],
                ar_ss.at[a, s, d - 1], ar_rs.at[a, s, d - 1], (to * NZ + z, i),
            )

        return make

    def rs_z(a, s):
        def make(d):
            to = along_z(d)
            return remote(
                z_src.at[a, s, pl.ds(pl.multiple_of(ZR * to, 16), ZR)], z_land.at[a, s, d - 1],
                ar_ss.at[a, s, 2 + d], ar_rs.at[a, s, 2 + d], (x * NZ + to, i),
            )

        return make

    def ag_z(a, s):
        def make(d):
            mine = z_all.at[a, s, pl.ds(pl.multiple_of(ZR * z, 16), ZR)]
            return remote(
                mine, mine, ar_ss.at[a, s, 9 + d], ar_rs.at[a, s, 9 + d], (x * NZ + along_z(d), i)
            )

        return make

    def ag_x(a, s):
        whole = d_st if a else st

        def make(d):
            return remote(
                z_all.at[a, s, pl.ds(0, XR)], whole.at[s, pl.ds(pl.multiple_of(XR * x, 16), XR)],
                ar_ss.at[a, s, 16 + d], ar_rs.at[a, s, 16 + d], (along_x(d) * NZ + z, i),
            )

        return make

    def start_x(a, s):
        launch(rs_x(a, s), 1, NX, ("rx", a, s))

    def x_to_z(a, s, fix):
        arrive(("rx", a, s))
        total = x_src[a, s, pl.ds(pl.multiple_of(XR * x, 16), XR), :].astype(F32)
        for d in range(NX - 1):
            total = total + x_land[a, s, d].astype(F32)
        z_src[a, s, :XR] = fix(total).astype(BF)
        launch(rs_z(a, s), 1, NZ, ("rz", a, s))

    def z_to_all(a, s, fix):
        arrive(("rz", a, s))
        total = z_src[a, s, pl.ds(pl.multiple_of(ZR * z, 16), ZR), :].astype(F32)
        for d in range(NZ - 1):
            total = total + z_land[a, s, d].astype(F32)
        z_all[a, s, pl.ds(pl.multiple_of(ZR * z, 16), ZR), :] = fix(total).astype(BF)
        launch(ag_z(a, s), 1, NZ, ("az", a, s))

    def all_to_x(a, s):
        arrive(("az", a, s))
        launch(ag_x(a, s), 1, NX, ("ax", a, s))
        whole = d_st if a else st
        whole[s, pl.ds(pl.multiple_of(XR * x, 16), XR), :] = z_all[a, s, :XR]

    def w_plane(d):
        return remote(w_mine, w_land.at[t], w_ss.at[d - 1], w_rs.at[d - 1], (plane(d), i))

    def tree(which):
        def make(ss, rs, src, dst, step):
            return remote(src, dst, ss.at[which], rs.at[which], (t, along_y(step) * 2 + c))

        return make

    def w_rows(away, first=0, count=COLS_IP):
        return w_t.at[pl.ds(pl.multiple_of(COLS_IP * (c * NY + along_y(away)) + first, 16), count)]

    def w_near(which):
        part = w_rows(0)
        return tree(which)(wy_ss, wy_rs, part, part, (1, 7, 2, 6)[which])

    def w_far(which):
        part = w_rows((6, 2)[which])
        return tree(4 + which)(wy_ss, wy_rs, part, part, (1, 7)[which])

    def w_half(which):
        part = (w_rows(6, PART, COLS_IP - PART), w_rows(2, 0, PART))[which]
        return tree(6 + which)(wy_ss, wy_rs, part, part, (2, 6)[which])

    def w_core(d):
        mine = w_t.at[group(c * NY + along_y(d))]
        return remote(mine, mine, wc_ss.at[d], wc_rs.at[d], sib)

    def band_core(d):
        return remote(core_src.at[d], core_land.at[d], c_ss.at[d], c_rs.at[d], sib)

    def b_tree(n):
        src, dst, step = (
            lambda: (y_src.at[1], y_land.at[0], 1),
            lambda: (y_src.at[7], y_land.at[1], 7),
            lambda: (y_mid.at[0], y_land.at[2], 2),
            lambda: (y_mid.at[1], y_land.at[3], 6),
            lambda: (y_src.at[3], y_far.at[0], 1),
            lambda: (y_src.at[5], y_far.at[1], 7),
            lambda: (y_src.at[4, pl.ds(0, PART)], y_far.at[2, pl.ds(0, PART)], 2),
            lambda: (y_src.at[4, pl.ds(PART, COLS_IP - PART)], y_far.at[2, pl.ds(PART, COLS_IP - PART)], 6),
        )[n]()
        return tree(n)(y_ss, y_rs, src, dst, step)

    def gate_core():
        return remote(g_core, g_core_land, g_ss.at[0], g_rs.at[0], sib)

    def gate_y(d):
        return remote(g_src.at[group(along_y(d))], g_land.at[d - 1], g_ss.at[d], g_rs.at[d], (t, along_y(d) * 2 + c))

    def halves(column):
        high = rounded(column)
        lane = lane_of((column.shape[0], LANES)) + (FP - LANES)
        return jnp.where(lane == F, high, jnp.where(lane == F + 1, column - high, 0.0))

    def add_halves(tile):
        at = F - FP + LANES
        return halves(tile[:, at : at + 1] + tile[:, at + 1 : at + 2])

    def hot_rows(b):
        shape = (ROWS_TP, FP)
        j, lane = row_of(shape), lane_of(shape)
        at = jnp.where(j < ROWS_T, ROWS_T * b + j, jnp.where(j < ROWS_T + 2, F - ROWS_T + j, -1))
        hot_f[pl.ds(pl.multiple_of(ROWS_TP * b, 16), ROWS_TP), :] = jnp.where(lane == at, 1.0, 0.0).astype(BF)

    def hot_cols(g):
        shape = (COLS_IP, DW)
        j, lane = row_of(shape), lane_of(shape)
        first = COLS_I * (2 * (g % NY) + g // NY)
        hot_d[group(g), :] = jnp.where(lane == jnp.where(j < COLS_I, first + j, -1), 1.0, 0.0).astype(BF)

    def to_groups(b):
        rows = pl.ds(pl.multiple_of(256 * b, 16), 256)
        hot = hot_d[rows, :]
        sc_cols[rows, :] = dot(hot, scaled[...], NTD).astype(BF)
        cot_cols[rows, :] = dot(hot, cot_ref[...], NTD).astype(BF)

    def ratios(s):
        cols = slice(TOK * s, TOK * s + TOK)
        for h in range(HEADS):
            rows = slice(HEAD * h, HEAD * h + HEAD)
            both = dot(st[s, rows, :], kq[s, rows, :], TN)
            one_over = 1.0 / (both[HEAD : HEAD + 1] + both[HEAD + 1 : HEAD + 2])
            inv[s, h] = one_over
            att[rows, cols] = (both[:HEAD] * one_over).astype(BF)

    def middle(s):
        cols = slice(TOK * s, TOK * s + TOK)
        for h in range(HEADS):
            rows = slice(HEAD * h, HEAD * h + HEAD)
            d_num = rounded(d_att[rows, cols] * inv[s, h])
            d_den = -jnp.sum(d_num * att[rows, cols].astype(F32), axis=0, keepdims=True)
            high = rounded(d_den)
            row = row_of((LANES - HEAD, TOK))
            rest = jnp.where(row < 2, high, jnp.where(row == 2, d_den - high, 0.0))
            dna[s, h, :HEAD] = d_num.astype(BF)
            dna[s, h, HEAD:] = rest.astype(BF)
            acc = dot(kq[s, rows, :], dna[s, h], NTD)
            x_src[1, s, rows, :] = jnp.where(lane_of(acc.shape) == HEAD + 1, 0.0, acc).astype(BF)

    def band(first):
        rows = pl.ds(pl.multiple_of(first, 16), COLS_IP)
        return dot(sc_cols[rows, :], att[...], NTD)

    def gate_tile(first):
        rows = pl.ds(pl.multiple_of(first, 16), HALF // 2)
        part = dot(w_t[rows, :], att[...], NN) * cot_cols[rows, :].astype(F32)
        return halves(jnp.sum(part, axis=1, keepdims=True))

    def last_grads(s):
        arrive(("ax", 1, s))
        for h in range(HEADS):
            rows = slice(HEAD * h, HEAD * h + HEAD)
            keys = kk[s, rows, :]
            state = d_st[s, rows, :]
            grad = dot(state, vs[s, h], NN)
            dk_ref[s, rows, :] = (grad * jnp.minimum(keys.astype(F32), 1.0)).astype(BF)
            dv_ref[s, rows, :] = dot(state, keys, TN)[:HEAD].astype(BF)

    def pieces(b):
        total = p_sum[...]
        rows = pl.ds(pl.multiple_of(ROWS_TP * 8 * b, 16), ROWS_TP * 8)
        p_src[pl.ds(8 * b, 8)] = dot(hot_f[rows, :], total, NTD).astype(BF).reshape(8, ROWS_TP, LANES)

    def p_plane(d):
        return remote(p_src.at[plane(d)], p_land.at[d - 1], p_ss.at[d - 1], p_rs.at[d - 1], (plane(d), i))

    for a in range(2):
        for s in range(2):
            x_src[a, s, F:] = jnp.zeros((NX * XR - F, LANES), BF)
            z_src[a, s, XR:] = jnp.zeros((NZ * ZR - XR, LANES), BF)
    att[F:, :] = jnp.zeros((FP - F, 2 * TOK), BF)
    p_sum[COLS_IP:, :] = jnp.zeros((LANES - COLS_IP, FP), BF)

    pl.semaphore_wait(barrier, NT - 1 + NY - 1 + 1)
    launch(w_plane, 1, NT, "w")
    loads[0].wait()
    loads[1].wait()
    state_part(0)
    start_x(0, 0)
    state_part(1)
    start_x(0, 1)
    w_land[t] = w_mine[...]
    loop(0, NT, hot_rows)
    x_to_z(0, 0, split_sum)
    x_to_z(0, 1, split_sum)

    arrive("w")
    for b in range(FP // 384):
        cols = slice(384 * b, 384 * b + 384)
        block = dot(w_land[...].reshape(NT * ROWS_TP, LANES), hot_f[:, cols], TN)
        w_t[group(c * NY + y), cols] = block[:COLS_IP].astype(BF)
    for n in (2, 3, 0, 1):
        w_near(n).start()
    w_core(0).start()
    z_to_all(0, 0, split_sum)
    z_to_all(0, 1, split_sum)
    loop(0, 2 * NY, hot_cols)

    loads[2].wait()
    for s in range(2):
        rows = slice(TOK * s, TOK * s + TOK)
        gate = table_ref[...].reshape(1, DW) + time_ref[s]
        scaled[rows, :] = ((LOSS_SCALE * gate) * cot_ref[rows, :].astype(F32)).astype(BF)
    loop(0, DP // 256, to_groups)

    w_near(2).wait_recv()
    w_far(0).start()
    w_half(0).start()
    w_core(6).start()
    w_near(3).wait_recv()
    w_far(1).start()
    w_half(1).start()
    w_core(2).start()
    w_near(0).wait_recv()
    w_core(7).start()
    w_near(1).wait_recv()
    w_core(1).start()
    all_to_x(0, 0)
    all_to_x(0, 1)
    loads[3].wait()
    for s in range(2):
        for h in range(HEADS):
            rows = slice(HEAD * h, HEAD * h + HEAD)
            kq[s, rows, :] = phi(q_ref[s, rows, :].astype(F32)).astype(BF)

    arrive(("ax", 0, 0))
    ratios(0)
    arrive(("ax", 0, 1))
    ratios(1)

    order = (3, 5, 4, 1, 7, 2, 6, 0)
    for d in order:
        core_src[d] = band(COLS_IP * ((1 - c) * NY + along_y(d))).astype(BF)
        band_core(d).start()
    for d in order:
        own_band[d] = band(COLS_IP * (c * NY + along_y(d)))
    after = {3: (4,), 5: (5,), 4: (6, 7), 1: (0,), 7: (1,)}
    for d in order:
        band_core(d).wait_recv()
        y_src[d] = (own_band[d] + core_land[d].astype(F32)).astype(BF)
        for n in after.get(d, ()):
            b_tree(n).start()

    w_far(0).wait_recv()
    w_core(5).start()
    w_far(1).wait_recv()
    w_core(3).start()
    w_half(0).wait_recv()
    w_half(1).wait_recv()
    w_core(4).start()
    loop(0, NY, lambda d: w_core(d).wait_recv())
    for b in range(FP // 384):
        cols = slice(384 * b, 384 * b + 384)
        d_att[cols, :] = dot(w_t[:, cols], sc_cols[...], TN)
    middle(0)
    start_x(1, 0)
    middle(1)
    start_x(1, 1)

    for b in range(2):
        rows = slice(HALF // 2 * b, HALF // 2 * (b + 1))
        g_core[rows, :] = gate_tile(HALF * (1 - c) + HALF // 2 * b).astype(BF)
    gate_core().start()

    b_tree(4).wait_recv()
    b_tree(6).wait_recv()
    y_mid[0] = (y_src[2].astype(F32) + y_far[0].astype(F32)).astype(BF)
    y_mid[0, :PART] = (
        y_src[2, :PART].astype(F32) + y_far[0, :PART].astype(F32) + y_far[2, :PART].astype(F32)
    ).astype(BF)
    b_tree(2).start()
    b_tree(5).wait_recv()
    b_tree(7).wait_recv()
    y_mid[1] = (y_src[6].astype(F32) + y_far[1].astype(F32)).astype(BF)
    y_mid[1, PART:] = (
        y_src[6, PART:].astype(F32) + y_far[1, PART:].astype(F32) + y_far[2, PART:].astype(F32)
    ).astype(BF)
    b_tree(3).start()

    x_to_z(1, 0, same)
    x_to_z(1, 1, same)
    gate_core().wait_recv()
    for b in range(2):
        rows = slice(HALF // 2 * b, HALF // 2 * (b + 1))
        part = gate_tile(HALF * c + HALF // 2 * b) + g_core_land[rows, :].astype(F32)
        g_src[rows, :] = add_halves(part).astype(BF)
    launch(gate_y, 1, NY, "g")
    for s in range(2):
        for h in range(HEADS):
            rows = slice(HEAD * h, HEAD * h + HEAD)
            grad = dot(st[s, rows, :], dna[s, h], NN)
            slope = jnp.minimum(kq[s, rows, :].astype(F32), 1.0)
            dq_ref[s, rows, :] = (grad * slope).astype(BF)
    z_to_all(1, 0, same)
    z_to_all(1, 1, same)

    for n in range(4):
        b_tree(n).wait_recv()
    total = y_src[0].astype(F32)
    for d in range(4):
        total = total + y_land[d].astype(F32)
    p_sum[:COLS_IP, :] = total.astype(BF)
    arrive("g")
    gate = g_src[group(y), :].astype(F32)
    for d in range(NY - 1):
        gate = gate + g_land[d].astype(F32)
    last = total[:, FP - LANES :] + add_halves(gate)
    p_sum[:COLS_IP, FP - LANES :] = last.astype(BF)
    loop(0, NT // 8, pieces)
    launch(p_plane, 1, NT, "p")
    all_to_x(1, 0)
    all_to_x(1, 1)

    last_grads(0)
    last_grads(1)
    arrive("p")
    total = p_src[t].astype(F32)
    for d in range(NT - 1):
        total = total + p_land[d].astype(F32)
    wg_ref[...] = total[:ROWS_T, :COLS_I] * (1.0 / LOSS_SCALE)
    gate_ref[...] = total[ROWS_T : ROWS_T + 1, :COLS_I] + total[ROWS_T + 1 : ROWS_T + 2, :COLS_I]

    drain()
    for n in range(4):
        w_near(n).wait_send()
    for n in range(2):
        w_far(n).wait_send()
        w_half(n).wait_send()
    loop(0, NY, lambda d: w_core(d).wait_send())
    loop(0, NY, lambda d: band_core(d).wait_send())
    for n in range(8):
        b_tree(n).wait_send()
    gate_core().wait_send()


def on_device(query_in, key_in, value_in, cotangent, out_weight, gate_table, time_gate):
    dma = pltpu.SemaphoreType.DMA
    vm = pltpu.VMEM
    whole = pl.BlockSpec(memory_space=pltpu.VMEM)
    turned = lambda a: jnp.swapaxes(a, 2, 3).reshape(2, F, TOK)
    out = pl.pallas_call(
        kernel,
        name="linear_attention_backward",
        out_shape=[jax.ShapeDtypeStruct((2, F, TOK), BF)] * 3
        + [jax.ShapeDtypeStruct((ROWS_T, COLS_I), F32), jax.ShapeDtypeStruct((1, COLS_I), F32)],
        in_specs=[pl.BlockSpec(memory_space=pltpu.HBM)] * 4 + [whole] * 3,
        out_specs=[whole] * 5,
        scratch_shapes=[
            vm((2, F, TOK), BF),
            vm((2, F, TOK), BF),
            vm((2, HEADS, LANES, TOK), BF),
            vm((NT * ROWS_TP, FP), BF),
            vm((DP, DW), BF),
            vm((2 * TOK, DW), BF),
            vm((DP, 2 * TOK), BF),
            vm((DP, 2 * TOK), BF),
            vm((ROWS_TP, LANES), BF),
            vm((NT, ROWS_TP, LANES), BF),
            vm((DP, FP), BF),
            vm((2, NX * XR, LANES), BF),
            vm((2, NX * XR, LANES), BF),
            vm((2, 2, NX * XR, LANES), BF),
            vm((2, 2, NX - 1, XR, LANES), BF),
            vm((2, 2, NZ * ZR, LANES), BF),
            vm((2, 2, NZ - 1, ZR, LANES), BF),
            vm((2, 2, NZ * ZR, LANES), BF),
            vm((FP, 2 * TOK), F32),
            vm((FP, 2 * TOK), BF),
            vm((2, HEADS, 1, TOK), F32),
            vm((2, HEADS, LANES, TOK), BF),
            vm((NY, COLS_IP, FP), BF),
            vm((NY, COLS_IP, FP), BF),
            vm((NY, COLS_IP, FP), F32),
            vm((NY, COLS_IP, FP), BF),
            vm((4, COLS_IP, FP), BF),
            vm((2, COLS_IP, FP), BF),
            vm((3, COLS_IP, FP), BF),
            vm((LANES, FP), BF),
            vm((NT, ROWS_TP, LANES), BF),
            vm((NT - 1, ROWS_TP, LANES), BF),
            vm((HALF, LANES), BF),
            vm((HALF, LANES), BF),
            vm((HALF, LANES), BF),
            vm((NY - 1, COLS_IP, LANES), BF),
            vm((2 * TOK, DW), BF),
            vm((2, F, TOK), BF),
            vm((2, F, TOK), BF),
            vm((2, F, TOK), BF),
            dma((NT - 1,)), dma((NT - 1,)),
            dma((8,)), dma((8,)),
            dma((NY,)), dma((NY,)),
            dma((2, 2, 20)), dma((2, 2, 20)),
            dma((NY,)), dma((NY,)),
            dma((8,)), dma((8,)),
            dma((NT - 1,)), dma((NT - 1,)),
            dma((NY,)), dma((NY,)), dma((4,)),
        ],
        compiler_params=pltpu.CompilerParams(
            collective_id=0, has_side_effects=True, vmem_limit_bytes=52 * 2**20
        ),
    )(
        turned(query_in),
        turned(key_in),
        turned(value_in),
        cotangent.reshape(2 * TOK, DW),
        out_weight,
        gate_table,
        time_gate,
    )
    back = lambda a: jnp.swapaxes(a.reshape(2, 1, F, TOK), 2, 3)
    return back(out[0]), back(out[1]), back(out[2]), out[4].reshape(COLS_I), out[3]


def solution(mesh):
    big = P(None, "img", "tok", None)
    return jax.shard_map(
        on_device,
        mesh=mesh,
        in_specs=(big, big, big, big, P("tok", "img"), P(), P(None, "img", None)),
        out_specs=(big, big, big, P("img"), P("tok", "img")),
        check_vma=False,
    )
```

time: 113 us -> 105 us (0.929)
  Pallas kernels: 107 us -> 98.6 us
    pallas_call x1, Pallas kernels: 107 us -> 98.6 us  [on_device(): pl.pallas_call(kernel, name='linear_attention_backward', out_shape=[jax.S...]
    unnamed x13 -> x11, local copies, waits for them, and re-layouts: 5.17 us -> 5.64 us
where the time goes in v3:
time: 105 us
  Pallas kernels  98.6 us (94%)
  local copies, waits for them, and re-layouts  5.64 us (5%)
    pallas_call x1, Pallas kernels, on_device(): pl.pallas_call(kernel, name='linear_attention_backward', out_shape=[jax.S...  98.6 us
    unnamed x11, local copies, waits for them, and re-layouts  5.64 us

profile of v3, /device:TPU:1, one launch (start us, length us, event | category | flops | bytes accessed | tf_op | source)
XLA Modules:
  0.0 104.9 jit_solution(3078079375452746918)
XLA Ops:
  0.6 0.0 copy-start
  0.6 0.7 copy-done
  1.3 0.0 copy-start.1
  1.3 0.7 copy-done.1
  2.0 0.0 copy-start.2
  2.0 0.7 copy-done.2
  2.7 98.6 %linear_attention_backward.1 = (bf16[2,1120,128]{2,1,0:T(8,128)(2,1)S(1)}, bf16[2,1120,128]{2,1,0:T(8,128)(2,1)S(1)}, bf16[2,1120,128]{2,1,0:T(8,128)(2,1)S(1)}, f32[35,72]{1,0:T(8,128)S(1)}, f32[1,72]{1,0:T(1,128)S(1)}) custom-call(bf16[2,1120,128]{2,1,0:T(8,128)(2,1)} %bitcast.37, bf16[2,1120,128]{2,1,0:T(8,128)(2,1)} %bitcast.38, ...), custom_call_target="tpu_custom_call" | custom-call | tf_op jit(solution)/shard_map/linear_attention_backward/pallas_call | solution.py:526
  101.3 0.8 copy.23
  102.1 0.8 copy.24
  102.9 0.8 copy.25
  103.8 0.5 copy.26
  104.3 0.6 copy.27
Async XLA Ops:
  0.6 0.7 copy-start
  1.3 0.7 copy-start.1
  2.0 0.7 copy-start.2

commit v4 on v3

--- a/solution.py
+++ b/solution.py
@@ -24,6 +24,8 @@
 XR = 288
 ZR = 48
 PART = 48
+CUT = 640
+EARLY = 18
 BF = jnp.bfloat16
 F32 = jnp.float32
 MESH = pl.DeviceIdType.MESH
@@ -73,12 +75,12 @@
 
 
 def kernel(
-    q_in, k_in, v_in, cot_in, w_ref, table_ref, time_ref,
+    q_in, k_in, v_in, cot_in, w_in, table_in, time_in,
     dq_ref, dk_ref, dv_ref, wg_ref, gate_ref,
     kq, kk, vs, hot_f, hot_d, scaled, sc_cols, cot_cols,
     w_mine, w_land, w_t, st, d_st, x_src, x_land, z_src, z_land, z_all,
-    d_att, att, inv, dna, core_src, core_land, own_band, y_src, y_land, y_mid, y_far, p_sum, p_src, p_land,
-    g_core, g_core_land, g_src, g_land, cot_ref, q_ref, k_ref, v_ref,
+    d_att, att, inv, dna, core_src, core_land, own_band, y_src, y_land, y_mid, y_far, p_sum, g_sum, p_src, p_land,
+    g_core, g_core_land, g_src, g_land, cot_ref, q_ref, k_ref, v_ref, w_ref, table_ref, time_ref,
     w_ss, w_rs, wy_ss, wy_rs, wc_ss, wc_rs, ar_ss, ar_rs, c_ss, c_rs, y_ss, y_rs, p_ss, p_rs, g_ss, g_rs, in_sem,
 ):
     t = lax.axis_index("tok")
@@ -127,10 +129,12 @@
 
     loads = [
         pltpu.make_async_copy(src, dst, in_sem.at[n])
-        for n, (src, dst) in enumerate(((k_in, k_ref), (v_in, v_ref), (cot_in, cot_ref), (q_in, q_ref)))
+        for n, (src, dst) in enumerate(
+            ((k_in, k_ref), (v_in, v_ref), (cot_in, cot_ref), (q_in, q_ref), (w_in, w_ref), (table_in, table_ref), (time_in, time_ref))
+        )
     ]
-    for load in loads:
-        load.start()
+    for n in (4, 0, 1, 2, 3, 5, 6):
+        loads[n].start()
     loop(1, NT, lambda d: greet((plane(d), i)))
     loop(1, NY, lambda d: greet((t, along_y(d) * 2 + c)))
     greet(sib)
@@ -142,7 +146,6 @@
         return pl.ds(pl.multiple_of(HEAD * h, 16), HEAD)
 
     w_mine[...] = jnp.zeros((ROWS_TP, LANES), BF)
-    w_mine[:ROWS_T, :COLS_I] = w_ref[...]
     ones = jnp.where(row_of((LANES - HEAD, TOK)) < 3, 1.0, 0.0).astype(BF)
 
     def state_part(s):
@@ -253,18 +256,20 @@
     def band_core(d):
         return remote(core_src.at[d], core_land.at[d], c_ss.at[d], c_rs.at[d], sib)
 
-    def b_tree(n):
-        src, dst, step = (
-            lambda: (y_src.at[1], y_land.at[0], 1),
-            lambda: (y_src.at[7], y_land.at[1], 7),
-            lambda: (y_mid.at[0], y_land.at[2], 2),
-            lambda: (y_mid.at[1], y_land.at[3], 6),
-            lambda: (y_src.at[3], y_far.at[0], 1),
-            lambda: (y_src.at[5], y_far.at[1], 7),
-            lambda: (y_src.at[4, pl.ds(0, PART)], y_far.at[2, pl.ds(0, PART)], 2),
-            lambda: (y_src.at[4, pl.ds(PART, COLS_IP - PART)], y_far.at[2, pl.ds(PART, COLS_IP - PART)], 6),
-        )[n]()
-        return tree(n)(y_ss, y_rs, src, dst, step)
+    def b_tree(n, half):
+        cols = pl.ds(CUT * half, FP - CUT if half else CUT)
+        every, front, back = pl.ds(0, COLS_IP), pl.ds(0, PART), pl.ds(PART, COLS_IP - PART)
+        src, dst, rows, step = (
+            (y_src.at[1], y_land.at[0], every, 1),
+            (y_src.at[7], y_land.at[1], every, 7),
+            (y_mid.at[0], y_land.at[2], every, 2),
+            (y_mid.at[1], y_land.at[3], every, 6),
+            (y_src.at[3], y_far.at[0], every, 1),
+            (y_src.at[5], y_far.at[1], every, 7),
+            (y_src.at[4], y_far.at[2], front, 2),
+            (y_src.at[4], y_far.at[2], back, 6),
+        )[n]
+        return tree(8 * half + n)(y_ss, y_rs, src.at[rows, cols], dst.at[rows, cols], step)
 
     def gate_core():
         return remote(g_core, g_core_land, g_ss.at[0], g_rs.at[0], sib)
@@ -341,11 +346,6 @@
             dk_ref[s, rows, :] = (grad * jnp.minimum(keys.astype(F32), 1.0)).astype(BF)
             dv_ref[s, rows, :] = dot(state, keys, TN)[:HEAD].astype(BF)
 
-    def pieces(b):
-        total = p_sum[...]
-        rows = pl.ds(pl.multiple_of(ROWS_TP * 8 * b, 16), ROWS_TP * 8)
-        p_src[pl.ds(8 * b, 8)] = dot(hot_f[rows, :], total, NTD).astype(BF).reshape(8, ROWS_TP, LANES)
-
     def p_plane(d):
         return remote(p_src.at[plane(d)], p_land.at[d - 1], p_ss.at[d - 1], p_rs.at[d - 1], (plane(d), i))
 
@@ -355,15 +355,18 @@
             z_src[a, s, XR:] = jnp.zeros((NZ * ZR - XR, LANES), BF)
     att[F:, :] = jnp.zeros((FP - F, 2 * TOK), BF)
     p_sum[COLS_IP:, :] = jnp.zeros((LANES - COLS_IP, FP), BF)
-
-    pl.semaphore_wait(barrier, NT - 1 + NY - 1 + 1)
-    launch(w_plane, 1, NT, "w")
+    g_sum[COLS_IP:, :] = jnp.zeros((LANES - COLS_IP, LANES), BF)
+
+    loads[4].wait()
+    w_mine[:ROWS_T, :COLS_I] = w_ref[...]
     loads[0].wait()
     loads[1].wait()
     state_part(0)
+    state_part(1)
+    pl.semaphore_wait(barrier, NT - 1 + NY - 1 + 1)
     start_x(0, 0)
-    state_part(1)
     start_x(0, 1)
+    launch(w_plane, 1, NT, "w")
     w_land[t] = w_mine[...]
     loop(0, NT, hot_rows)
     x_to_z(0, 0, split_sum)
@@ -382,6 +385,8 @@
     loop(0, 2 * NY, hot_cols)
 
     loads[2].wait()
+    loads[5].wait()
+    loads[6].wait()
     for s in range(2):
         rows = slice(TOK * s, TOK * s + TOK)
         gate = table_ref[...].reshape(1, DW) + time_ref[s]
@@ -419,12 +424,18 @@
         band_core(d).start()
     for d in order:
         own_band[d] = band(COLS_IP * (c * NY + along_y(d)))
-    after = {3: (4,), 5: (5,), 4: (6, 7), 1: (0,), 7: (1,)}
+    after = {
+        3: ((4, 0),),
+        5: ((5, 0),),
+        4: ((6, 0), (7, 0), (4, 1), (5, 1), (6, 1), (7, 1)),
+        1: ((0, 0),),
+        7: ((1, 0), (0, 1), (1, 1)),
+    }
     for d in order:
         band_core(d).wait_recv()
         y_src[d] = (own_band[d] + core_land[d].astype(F32)).astype(BF)
-        for n in after.get(d, ()):
-            b_tree(n).start()
+        for n, half in after.get(d, ()):
+            b_tree(n, half).start()
 
     w_far(0).wait_recv()
     w_core(5).start()
@@ -442,25 +453,20 @@
     middle(1)
     start_x(1, 1)
 
+    for half in range(2):
+        cols = slice(CUT * half, FP if half else CUT)
+        for n, near, rows in ((0, 2, slice(0, PART)), (1, 6, slice(PART, COLS_IP))):
+            b_tree(4 + n, half).wait_recv()
+            b_tree(6 + n, half).wait_recv()
+            part = y_src[near, :, cols].astype(F32) + y_far[n, :, cols].astype(F32)
+            y_mid[n, :, cols] = part.astype(BF)
+            y_mid[n, rows, cols] = (part[rows] + y_far[2, rows, cols].astype(F32)).astype(BF)
+            b_tree(2 + n, half).start()
+
     for b in range(2):
         rows = slice(HALF // 2 * b, HALF // 2 * (b + 1))
         g_core[rows, :] = gate_tile(HALF * (1 - c) + HALF // 2 * b).astype(BF)
     gate_core().start()
-
-    b_tree(4).wait_recv()
-    b_tree(6).wait_recv()
-    y_mid[0] = (y_src[2].astype(F32) + y_far[0].astype(F32)).astype(BF)
-    y_mid[0, :PART] = (
-        y_src[2, :PART].astype(F32) + y_far[0, :PART].astype(F32) + y_far[2, :PART].astype(F32)
-    ).astype(BF)
-    b_tree(2).start()
-    b_tree(5).wait_recv()
-    b_tree(7).wait_recv()
-    y_mid[1] = (y_src[6].astype(F32) + y_far[1].astype(F32)).astype(BF)
-    y_mid[1, PART:] = (
-        y_src[6, PART:].astype(F32) + y_far[1, PART:].astype(F32) + y_far[2, PART:].astype(F32)
-    ).astype(BF)
-    b_tree(3).start()
 
     x_to_z(1, 0, same)
     x_to_z(1, 1, same)
@@ -479,20 +485,46 @@
     z_to_all(1, 0, same)
     z_to_all(1, 1, same)
 
-    for n in range(4):
-        b_tree(n).wait_recv()
-    total = y_src[0].astype(F32)
-    for d in range(4):
-        total = total + y_land[d].astype(F32)
-    p_sum[:COLS_IP, :] = total.astype(BF)
+    def y_total(half):
+        cols = slice(CUT * half, FP if half else CUT)
+        for n in range(4):
+            b_tree(n, half).wait_recv()
+        total = y_src[0, :, cols].astype(F32)
+        for d in range(4):
+            total = total + y_land[d, :, cols].astype(F32)
+        p_sum[:COLS_IP, cols] = total.astype(BF)
+
+    def send_piece(to):
+        @pl.when(to != t)
+        def _():
+            p_plane(lax.rem(to - t + NT, NT)).start()
+
+    y_total(0)
     arrive("g")
     gate = g_src[group(y), :].astype(F32)
     for d in range(NY - 1):
         gate = gate + g_land[d].astype(F32)
-    last = total[:, FP - LANES :] + add_halves(gate)
-    p_sum[:COLS_IP, FP - LANES :] = last.astype(BF)
-    loop(0, NT // 8, pieces)
-    launch(p_plane, 1, NT, "p")
+    g_sum[:COLS_IP, :] = add_halves(gate).astype(BF)
+
+    def early(b):
+        rows = pl.ds(pl.multiple_of(ROWS_TP * 6 * b, 16), ROWS_TP * 6)
+        block = dot(hot_f[rows, :CUT], p_sum[:, :CUT], NTD) + dot(hot_f[rows, FP - LANES :], g_sum[...], NTD)
+        p_src[pl.ds(6 * b, 6)] = block.astype(BF).reshape(6, ROWS_TP, LANES)
+
+    loop(0, EARLY // 6, early)
+    loop(0, EARLY, send_piece)
+    y_total(1)
+    p_sum[:COLS_IP, FP - LANES :] = p_sum[:COLS_IP, FP - LANES :] + g_sum[:COLS_IP, :]
+
+    def late(b):
+        rows = pl.ds(pl.multiple_of(ROWS_TP * (EARLY + 7 * b), 16), ROWS_TP * 7)
+        block = dot(hot_f[rows, CUT - LANES :], p_sum[:, CUT - LANES :], NTD)
+        p_src[pl.ds(EARLY + 7 * b, 7)] = block.astype(BF).reshape(7, ROWS_TP, LANES)
+
+    loop(0, (NT - EARLY) // 7, late)
+    loop(EARLY, NT, send_piece)
+    sends.append((p_plane, 1, NT))
+    recvs["p"] = (p_plane, 1, NT)
     all_to_x(1, 0)
     all_to_x(1, 1)
 
@@ -514,7 +546,8 @@
     loop(0, NY, lambda d: w_core(d).wait_send())
     loop(0, NY, lambda d: band_core(d).wait_send())
     for n in range(8):
-        b_tree(n).wait_send()
+        for half in range(2):
+            b_tree(n, half).wait_send()
     gate_core().wait_send()
 
 
@@ -528,7 +561,7 @@
         name="linear_attention_backward",
         out_shape=[jax.ShapeDtypeStruct((2, F, TOK), BF)] * 3
         + [jax.ShapeDtypeStruct((ROWS_T, COLS_I), F32), jax.ShapeDtypeStruct((1, COLS_I), F32)],
-        in_specs=[pl.BlockSpec(memory_space=pltpu.HBM)] * 4 + [whole] * 3,
+        in_specs=[pl.BlockSpec(memory_space=pltpu.HBM)] * 7,
         out_specs=[whole] * 5,
         scratch_shapes=[
             vm((2, F, TOK), BF),
@@ -561,6 +594,7 @@
             vm((2, COLS_IP, FP), BF),
             vm((3, COLS_IP, FP), BF),
             vm((LANES, FP), BF),
+            vm((LANES, LANES), BF),
             vm((NT, ROWS_TP, LANES), BF),
             vm((NT - 1, ROWS_TP, LANES), BF),
             vm((HALF, LANES), BF),
@@ -571,14 +605,17 @@
             vm((2, F, TOK), BF),
             vm((2, F, TOK), BF),
             vm((2, F, TOK), BF),
+            vm((ROWS_T, COLS_I), BF),
+            vm((DW,), F32),
+            vm((2, 1, DW), F32),
             dma((NT - 1,)), dma((NT - 1,)),
             dma((8,)), dma((8,)),
             dma((NY,)), dma((NY,)),
             dma((2, 2, 20)), dma((2, 2, 20)),
             dma((NY,)), dma((NY,)),
-            dma((8,)), dma((8,)),
+            dma((16,)), dma((16,)),
             dma((NT - 1,)), dma((NT - 1,)),
-            dma((NY,)), dma((NY,)), dma((4,)),
+            dma((NY,)), dma((NY,)), dma((7,)),
         ],
         compiler_params=pltpu.CompilerParams(
             collective_id=0, has_side_effects=True, vmem_limit_bytes=52 * 2**20

time: 105 us -> 104 us (level)
  Pallas kernels: 98.6 us -> 97 us
    pallas_call x1, Pallas kernels: 98.6 us -> 97 us  [on_device(): pl.pallas_call(kernel, name='linear_attention_backward', out_shape=[jax.S...]
where the time goes in v4:
time: 104 us; the launch traced here: 103 us
  Pallas kernels  97 us (93%)
  local copies, waits for them, and re-layouts  5.64 us (5%)
    pallas_call x1, Pallas kernels, on_device(): pl.pallas_call(kernel, name='linear_attention_backward', out_shape=[jax.S...  97 us
    unnamed x11, local copies, waits for them, and re-layouts  5.64 us

profile of v4, /device:TPU:1, one launch (start us, length us, event | category | flops | bytes accessed | tf_op | source)
XLA Modules:
  0.0 103.2 jit_solution(12166375216352224158)
XLA Ops:
  0.6 0.0 copy-start
  0.6 0.7 copy-done
  1.3 0.0 copy-start.1
  1.3 0.7 copy-done.1
  2.0 0.0 copy-start.2
  2.0 0.7 copy-done.2
  2.7 97.0 %linear_attention_backward.1 = (bf16[2,1120,128]{2,1,0:T(8,128)(2,1)S(1)}, bf16[2,1120,128]{2,1,0:T(8,128)(2,1)S(1)}, bf16[2,1120,128]{2,1,0:T(8,128)(2,1)S(1)}, f32[35,72]{1,0:T(8,128)S(1)}, f32[1,72]{1,0:T(1,128)S(1)}) custom-call(bf16[2,1120,128]{2,1,0:T(8,128)(2,1)} %bitcast.37, bf16[2,1120,128]{2,1,0:T(8,128)(2,1)} %bitcast.38, ...), custom_call_target="tpu_custom_call" | custom-call | tf_op jit(solution)/shard_map/linear_attention_backward/pallas_call | solution.py:559
  99.7 0.8 copy.23
  100.5 0.8 copy.24
  101.3 0.8 copy.25
  102.1 0.5 copy.26
  102.6 0.6 copy.27
Async XLA Ops:
  0.6 0.7 copy-start
  1.3 0.7 copy-start.1
  2.0 0.7 copy-start.2

commit v5 on v4

--- a/solution.py
+++ b/solution.py
@@ -116,9 +116,7 @@
         make, first, last = recvs.pop(key)
         loop(first, last, lambda d: make(d).wait_recv())
 
-    def drain():
-        for key in list(recvs):
-            arrive(key)
+    def drain_sends():
         for make, first, last in sends:
             loop(first, last, lambda d: make(d).wait_send())
 
@@ -135,8 +133,10 @@
     ]
     for n in (4, 0, 1, 2, 3, 5, 6):
         loads[n].start()
-    loop(1, NT, lambda d: greet((plane(d), i)))
-    loop(1, NY, lambda d: greet((t, along_y(d) * 2 + c)))
+    for d in range(1, NT):
+        greet((plane(d), i))
+    for d in range(1, NY):
+        greet((t, along_y(d) * 2 + c))
     greet(sib)
 
     def group(g):
@@ -524,20 +524,12 @@
     loop(0, (NT - EARLY) // 7, late)
     loop(EARLY, NT, send_piece)
     sends.append((p_plane, 1, NT))
-    recvs["p"] = (p_plane, 1, NT)
     all_to_x(1, 0)
     all_to_x(1, 1)
 
     last_grads(0)
     last_grads(1)
-    arrive("p")
-    total = p_src[t].astype(F32)
-    for d in range(NT - 1):
-        total = total + p_land[d].astype(F32)
-    wg_ref[...] = total[:ROWS_T, :COLS_I] * (1.0 / LOSS_SCALE)
-    gate_ref[...] = total[ROWS_T : ROWS_T + 1, :COLS_I] + total[ROWS_T + 1 : ROWS_T + 2, :COLS_I]
-
-    drain()
+    drain_sends()
     for n in range(4):
         w_near(n).wait_send()
     for n in range(2):
@@ -549,6 +541,14 @@
         for half in range(2):
             b_tree(n, half).wait_send()
     gate_core().wait_send()
+
+    for d in range(1, NT):
+        p_plane(d).wait_recv()
+    total = p_src[t].astype(F32)
+    for d in range(NT - 1):
+        total = total + p_land[d].astype(F32)
+    wg_ref[...] = total[:ROWS_T, :COLS_I] * (1.0 / LOSS_SCALE)
+    gate_ref[...] = total[ROWS_T : ROWS_T + 1, :COLS_I] + total[ROWS_T + 1 : ROWS_T + 2, :COLS_I]
 
 
 def on_device(query_in, key_in, value_in, cotangent, out_weight, gate_table, time_gate):

time: 104 us -> 104 us (level)
  no operation moved by 1% of the time
where the time goes in v5:
time: 104 us; the launch traced here: 103 us
  Pallas kernels  96.7 us (93%)
  local copies, waits for them, and re-layouts  5.64 us (5%)
    pallas_call x1, Pallas kernels, on_device(): pl.pallas_call(kernel, name='linear_attention_backward', out_shape=[jax.S...  96.7 us
    unnamed x11, local copies, waits for them, and re-layouts  5.64 us

profile of v5, /device:TPU:1, one launch (start us, length us, event | category | flops | bytes accessed | tf_op | source)
XLA Modules:
  0.0 103.0 jit_solution(2130275653752171487)
XLA Ops:
  0.6 0.0 copy-start
  0.6 0.7 copy-done
  1.3 0.0 copy-start.1
  1.3 0.7 copy-done.1
  2.0 0.0 copy-start.2
  2.0 0.7 copy-done.2
  2.7 96.7 %linear_attention_backward.1 = (bf16[2,1120,128]{2,1,0:T(8,128)(2,1)S(1)}, bf16[2,1120,128]{2,1,0:T(8,128)(2,1)S(1)}, bf16[2,1120,128]{2,1,0:T(8,128)(2,1)S(1)}, f32[35,72]{1,0:T(8,128)S(1)}, f32[1,72]{1,0:T(1,128)S(1)}) custom-call(bf16[2,1120,128]{2,1,0:T(8,128)(2,1)} %bitcast.37, bf16[2,1120,128]{2,1,0:T(8,128)(2,1)} %bitcast.38, ...), custom_call_target="tpu_custom_call" | custom-call | tf_op jit(solution)/shard_map/linear_attention_backward/pallas_call | solution.py:559
  99.5 0.8 copy.23
  100.3 0.8 copy.24
  101.1 0.8 copy.25
  101.9 0.5 copy.26
  102.4 0.6 copy.27
Async XLA Ops:
  0.6 0.7 copy-start
  1.3 0.7 copy-start.1
  2.0 0.7 copy-start.2
